TPU v7x, 32 devices: a whole 2x2x4 slice. The times are simulated.
32 devices in a mesh: ctx: 16 (over z, x, core), head: 2 (over y).
Axes of the slice: x: 2, y: 2, z: 4, core: 2. Of those that a mesh axis runs over, the one named last changes fastest.
Arguments:
- query_rows: bfloat16 [3072, 8192], P('ctx', 'head'), may hold values from -6 to 6
- key_rows: bfloat16 [3072, 1024], P('ctx', 'head'), may hold values from -6 to 6
- value_rows: bfloat16 [3072, 1024], P('ctx', 'head'), may hold values from -6 to 6
- attn_output: bfloat16 [3072, 8192], P('ctx', 'head'), may hold values from -6 to 6
- log_norms: float32 [64, 3072], P('head', 'ctx'), may hold values from 3 to 5
- grad_output: bfloat16 [3072, 8192], P(('ctx', 'head')), may hold values from -2.390625 to 2.390625
- span_order: int32 [32], replicated, may hold values from 0 to 31, each once
Outputs:
- grad_query: bfloat16 [3072, 8192], P(('ctx', 'head'))
- grad_key: bfloat16 [3072, 1024], P('ctx', 'head')
- grad_value: bfloat16 [3072, 1024], P('ctx', 'head')
Inputs may be any that keep to these rules, and one draw needn't show every extreme that they name: span_order is a permutation: each of the 32 spans of 96 positions is held by exactly one slot.
All inputs are finite; a program needn't handle non-finite values.
Results may differ from a plain program's by a relative error of at most 0.0051.
Values may be sent and summed in bfloat16 or wider, within the bound.
A program may use at most 192 MiB of HBM per device.

v0:
```python
import jax
import jax.numpy as jnp
from jax import lax
from jax.sharding import PartitionSpec as P

QH = 64
KVH = 8
HD = 128


def passed_along(block, axis, distance):
    devices = range(lax.axis_size(axis))
    route = [((i - distance) % len(devices), i) for i in devices]
    return lax.ppermute(block, axis, route)


def table_positions(span_order, first_row, row_count, half_span):
    row_ids = first_row + jnp.arange(row_count, dtype=jnp.int32)
    slot_ids = row_ids // half_span
    slot_match = slot_ids[:, None] == jnp.arange(span_order.shape[0], dtype=jnp.int32)[None, :]
    span_ids = jnp.sum(jnp.where(slot_match, span_order[None, :], 0), axis=1)
    return span_ids * half_span + row_ids % half_span


def attend_block(
    query_heads, grad_heads, lse_rows, row_delta, query_pos, key_block, value_block, key_pos
):
    inv_root = query_heads.shape[-1] ** (-0.5)
    scores = (
        jnp.einsum("tngd,snd->tngs", query_heads, key_block, preferred_element_type=jnp.float32)
        * inv_root
    )
    causal = query_pos[:, None, None, None] >= key_pos[None, None, None, :]
    prob_full = jnp.where(causal, jnp.exp(scores - lse_rows[..., None]), 0.0)
    prob_low = prob_full.astype(jnp.bfloat16)
    dprobs = jnp.einsum(
        "tngd,snd->tngs", grad_heads, value_block, preferred_element_type=jnp.float32
    )
    dscores = (prob_full * (dprobs - row_delta[..., None])).astype(jnp.bfloat16)
    grad_q = (
        jnp.einsum("tngs,snd->tngd", dscores, key_block, preferred_element_type=jnp.float32)
        * inv_root
    )
    grad_k = (
        jnp.einsum("tngs,tngd->snd", dscores, query_heads, preferred_element_type=jnp.float32)
        * inv_root
    )
    grad_v = jnp.einsum("tngs,tngd->snd", prob_low, grad_heads, preferred_element_type=jnp.float32)
    return (grad_q, grad_k, grad_v)


def per_device(query_rows, key_rows, value_rows, attn_output, log_norms, grad_output, span_order):
    grad_rows = lax.all_to_all(grad_output, "head", split_axis=1, concat_axis=0, tiled=True)
    row_count = query_rows.shape[0]
    half_span = row_count // 2
    head_dim = HD
    kv_heads = key_rows.shape[1] // head_dim
    groups = QH // KVH
    query_heads = query_rows.reshape(row_count, kv_heads, groups, head_dim)
    grad_heads = grad_rows.reshape(row_count, kv_heads, groups, head_dim)
    out_heads = attn_output.reshape(row_count, kv_heads, groups, head_dim)
    row_delta = jnp.sum(grad_heads.astype(jnp.float32) * out_heads.astype(jnp.float32), axis=-1)
    lse_rows = log_norms.reshape(kv_heads, groups, row_count).transpose(2, 0, 1)
    cycle_size = lax.axis_size("ctx")
    device = lax.axis_index("ctx")
    query_pos = table_positions(span_order, device * row_count, row_count, half_span)

    def attend(key_block, value_block, key_pos):
        return attend_block(
            query_heads, grad_heads, lse_rows, row_delta, query_pos, key_block, value_block, key_pos
        )

    def block_terms(key_block, value_block, key_pos):
        return attend(key_block, value_block, key_pos)

    key_heads = key_rows.reshape(row_count, kv_heads, head_dim)
    value_heads = value_rows.reshape(row_count, kv_heads, head_dim)
    dq_init = jnp.zeros((row_count, kv_heads, groups, head_dim), jnp.float32)
    acc_init = jnp.zeros((row_count, kv_heads, head_dim), jnp.float32)

    def cycle_turn(turn_index, carry_state):
        key_block, value_block, dk_acc, dv_acc, dq_acc = carry_state
        source = (device - turn_index) % cycle_size
        key_pos = table_positions(span_order, source * row_count, row_count, half_span)
        grad_q, grad_k, grad_v = block_terms(key_block, value_block, key_pos)
        key_block, value_block = passed_along((key_block, value_block), "ctx", 1)
        dk_acc, dv_acc = passed_along((dk_acc + grad_k, dv_acc + grad_v), "ctx", 1)
        return (key_block, value_block, dk_acc, dv_acc, dq_acc + grad_q)

    key_block, value_block, dk_acc, dv_acc, dq_acc = lax.fori_loop(
        0, cycle_size - 1, cycle_turn, (key_heads, value_heads, acc_init, acc_init, dq_init)
    )
    source = (device + 1) % cycle_size
    key_pos = table_positions(span_order, source * row_count, row_count, half_span)
    grad_q, grad_k, grad_v = block_terms(key_block, value_block, key_pos)
    dq_acc = dq_acc + grad_q
    dk_mine, dv_mine = (
        passed_along((dk_acc + grad_k).astype(jnp.bfloat16), "ctx", 1).astype(jnp.float32),
        passed_along((dv_acc + grad_v).astype(jnp.bfloat16), "ctx", 1).astype(jnp.float32),
    )
    grad_local = dq_acc.reshape(row_count, kv_heads * groups * head_dim).astype(jnp.bfloat16)
    grad_query = lax.all_to_all(grad_local, "head", split_axis=0, concat_axis=1, tiled=True)
    grad_key = dk_mine.reshape(row_count, kv_heads * head_dim).astype(jnp.bfloat16)
    grad_value = dv_mine.reshape(row_count, kv_heads * head_dim).astype(jnp.bfloat16)
    return (grad_query, grad_key, grad_value)


def solution(mesh):
    return jax.shard_map(
        per_device,
        mesh=mesh,
        in_specs=(
            P("ctx", "head"),
            P("ctx", "head"),
            P("ctx", "head"),
            P("ctx", "head"),
            P("head", "ctx"),
            P(("ctx", "head"), None),
            P(),
        ),
        out_specs=(P(("ctx", "head"), None), P("ctx", "head"), P("ctx", "head")),
        check_vma=False,
    )
```

profile of v0, /device:TPU:9, one launch (start us, length us, event | category | flops | bytes accessed | tf_op | source)
XLA Modules:
  0.0 471.4 jit_solution(18428520251121545383)
XLA Ops:
  3.4 3.7 all-to-all-start
  18.2 7.5 %all-to-all-done = bf16[96,2,4096]{2,0,1:T(8,128)(2,1)S(1)} async-done(((bf16[96,2,4096]{2,0,1:T(8,128)(2,1)}), bf16[96,2,4096]{2,0,1:T(8,128)(2,1)S(1)}, u32[]{:S(2)}, u32[]{:S(2)}) %all-to-all-start) | async-done | bytes 1572896 | tf_op jit(solution)/shard_map/all_to_all | solution.py:53
  32.3 398.5 %while.25 = (s32[]{:T(128)}, bf16[192,4,128]{2,0,1:T(8,128)(2,1)}, bf16[192,4,128]{2,0,1:T(8,128)(2,1)}, f32[192,4,128]{2,0,1:T(8,128)}, f32[192,4,128]{2,0,1:T(...) while((s32[]{:T(128)}, bf16[192,4,128]{2,0,1:T(8,128)(2,1)}, ...), condition=%wide.region_4.5_spmd.clone, body=%wide.region_2.4_spmd.clone.sunk | while | flops 1524458752 | bytes 65464292 | solution.py:90
  50.5 4.0 copy.114
  54.5 4.7 bitcast_add_fusion.3
  76.4 4.0 copy.114
  80.4 5.7 %bitcast_add_fusion.3 = f32[192,4,8,128]{3,2,0,1:T(8,128)} fusion(f32[192,4,8,128]{3,2,0,1:T(8,128)} %get-tuple-element.592, bf16[192,4,8,192]{3,2,0,1:T(8,128)(2,1)} %copy.114, pred[]{:T(512)S(6)} %compare.6, bf16[192,4,128]{2,0,1:T(8,128)(2,1)S(1)} %copy.122), kind=kOutput, calls=%fused_computation.7.clone.1 | convolution fusion | flops 304349184 | bytes 8847361 | tf_op jit(solution)/shard_map/while/body/eval_jaxpr/tngs,snd->tngd/dot_general | solution.py:41
  101.9 4.0 copy.114
  105.9 5.6 %bitcast_add_fusion.3 = f32[192,4,8,128]{3,2,0,1:T(8,128)} fusion(f32[192,4,8,128]{3,2,0,1:T(8,128)} %get-tuple-element.592, bf16[192,4,8,192]{3,2,0,1:T(8,128)(2,1)} %copy.114, pred[]{:T(512)S(6)} %compare.6, bf16[192,4,128]{2,0,1:T(8,128)(2,1)S(1)} %copy.122), kind=kOutput, calls=%fused_computation.7.clone.1 | convolution fusion | flops 304349184 | bytes 8847361 | tf_op jit(solution)/shard_map/while/body/eval_jaxpr/tngs,snd->tngd/dot_general | solution.py:41
  125.7 3.6 fusion.105
  129.3 4.0 copy.114
  133.2 5.6 %bitcast_add_fusion.3 = f32[192,4,8,128]{3,2,0,1:T(8,128)} fusion(f32[192,4,8,128]{3,2,0,1:T(8,128)} %get-tuple-element.592, bf16[192,4,8,192]{3,2,0,1:T(8,128)(2,1)} %copy.114, pred[]{:T(512)S(6)} %compare.6, bf16[192,4,128]{2,0,1:T(8,128)(2,1)S(1)} %copy.122), kind=kOutput, calls=%fused_computation.7.clone.1 | convolution fusion | flops 304349184 | bytes 8847361 | tf_op jit(solution)/shard_map/while/body/eval_jaxpr/tngs,snd->tngd/dot_general | solution.py:41
  152.1 3.6 fusion.105
  155.7 4.0 copy.114
  159.6 5.6 %bitcast_add_fusion.3 = f32[192,4,8,128]{3,2,0,1:T(8,128)} fusion(f32[192,4,8,128]{3,2,0,1:T(8,128)} %get-tuple-element.592, bf16[192,4,8,192]{3,2,0,1:T(8,128)(2,1)} %copy.114, pred[]{:T(512)S(6)} %compare.6, bf16[192,4,128]{2,0,1:T(8,128)(2,1)S(1)} %copy.122), kind=kOutput, calls=%fused_computation.7.clone.1 | convolution fusion | flops 304349184 | bytes 8847361 | tf_op jit(solution)/shard_map/while/body/eval_jaxpr/tngs,snd->tngd/dot_general | solution.py:41
  179.0 3.6 fusion.105
  182.5 4.0 copy.114
  186.5 5.6 %bitcast_add_fusion.3 = f32[192,4,8,128]{3,2,0,1:T(8,128)} fusion(f32[192,4,8,128]{3,2,0,1:T(8,128)} %get-tuple-element.592, bf16[192,4,8,192]{3,2,0,1:T(8,128)(2,1)} %copy.114, pred[]{:T(512)S(6)} %compare.6, bf16[192,4,128]{2,0,1:T(8,128)(2,1)S(1)} %copy.122), kind=kOutput, calls=%fused_computation.7.clone.1 | convolution fusion | flops 304349184 | bytes 8847361 | tf_op jit(solution)/shard_map/while/body/eval_jaxpr/tngs,snd->tngd/dot_general | solution.py:41
  205.3 3.6 fusion.105
  208.9 4.0 copy.114
  212.9 5.6 %bitcast_add_fusion.3 = f32[192,4,8,128]{3,2,0,1:T(8,128)} fusion(f32[192,4,8,128]{3,2,0,1:T(8,128)} %get-tuple-element.592, bf16[192,4,8,192]{3,2,0,1:T(8,128)(2,1)} %copy.114, pred[]{:T(512)S(6)} %compare.6, bf16[192,4,128]{2,0,1:T(8,128)(2,1)S(1)} %copy.122), kind=kOutput, calls=%fused_computation.7.clone.1 | convolution fusion | flops 304349184 | bytes 8847361 | tf_op jit(solution)/shard_map/while/body/eval_jaxpr/tngs,snd->tngd/dot_general | solution.py:41
  231.8 3.6 fusion.105
  235.4 4.0 copy.114
  239.3 5.6 %bitcast_add_fusion.3 = f32[192,4,8,128]{3,2,0,1:T(8,128)} fusion(f32[192,4,8,128]{3,2,0,1:T(8,128)} %get-tuple-element.592, bf16[192,4,8,192]{3,2,0,1:T(8,128)(2,1)} %copy.114, pred[]{:T(512)S(6)} %compare.6, bf16[192,4,128]{2,0,1:T(8,128)(2,1)S(1)} %copy.122), kind=kOutput, calls=%fused_computation.7.clone.1 | convolution fusion | flops 304349184 | bytes 8847361 | tf_op jit(solution)/shard_map/while/body/eval_jaxpr/tngs,snd->tngd/dot_general | solution.py:41
  258.2 3.6 fusion.105
  261.8 4.0 copy.114
  265.8 5.6 %bitcast_add_fusion.3 = f32[192,4,8,128]{3,2,0,1:T(8,128)} fusion(f32[192,4,8,128]{3,2,0,1:T(8,128)} %get-tuple-element.592, bf16[192,4,8,192]{3,2,0,1:T(8,128)(2,1)} %copy.114, pred[]{:T(512)S(6)} %compare.6, bf16[192,4,128]{2,0,1:T(8,128)(2,1)S(1)} %copy.122), kind=kOutput, calls=%fused_computation.7.clone.1 | convolution fusion | flops 304349184 | bytes 8847361 | tf_op jit(solution)/shard_map/while/body/eval_jaxpr/tngs,snd->tngd/dot_general | solution.py:41
  285.1 3.6 fusion.105
  288.6 4.0 copy.114
  292.6 5.6 %bitcast_add_fusion.3 = f32[192,4,8,128]{3,2,0,1:T(8,128)} fusion(f32[192,4,8,128]{3,2,0,1:T(8,128)} %get-tuple-element.592, bf16[192,4,8,192]{3,2,0,1:T(8,128)(2,1)} %copy.114, pred[]{:T(512)S(6)} %compare.6, bf16[192,4,128]{2,0,1:T(8,128)(2,1)S(1)} %copy.122), kind=kOutput, calls=%fused_computation.7.clone.1 | convolution fusion | flops 304349184 | bytes 8847361 | tf_op jit(solution)/shard_map/while/body/eval_jaxpr/tngs,snd->tngd/dot_general | solution.py:41
  315.0 4.0 copy.114
  319.0 5.6 %bitcast_add_fusion.3 = f32[192,4,8,128]{3,2,0,1:T(8,128)} fusion(f32[192,4,8,128]{3,2,0,1:T(8,128)} %get-tuple-element.592, bf16[192,4,8,192]{3,2,0,1:T(8,128)(2,1)} %copy.114, pred[]{:T(512)S(6)} %compare.6, bf16[192,4,128]{2,0,1:T(8,128)(2,1)S(1)} %copy.122), kind=kOutput, calls=%fused_computation.7.clone.1 | convolution fusion | flops 304349184 | bytes 8847361 | tf_op jit(solution)/shard_map/while/body/eval_jaxpr/tngs,snd->tngd/dot_general | solution.py:41
  337.9 3.6 fusion.105
  341.5 4.0 copy.114
  345.5 5.6 %bitcast_add_fusion.3 = f32[192,4,8,128]{3,2,0,1:T(8,128)} fusion(f32[192,4,8,128]{3,2,0,1:T(8,128)} %get-tuple-element.592, bf16[192,4,8,192]{3,2,0,1:T(8,128)(2,1)} %copy.114, pred[]{:T(512)S(6)} %compare.6, bf16[192,4,128]{2,0,1:T(8,128)(2,1)S(1)} %copy.122), kind=kOutput, calls=%fused_computation.7.clone.1 | convolution fusion | flops 304349184 | bytes 8847361 | tf_op jit(solution)/shard_map/while/body/eval_jaxpr/tngs,snd->tngd/dot_general | solution.py:41
  364.3 3.6 fusion.105
  367.9 4.0 copy.114
  371.9 5.6 %bitcast_add_fusion.3 = f32[192,4,8,128]{3,2,0,1:T(8,128)} fusion(f32[192,4,8,128]{3,2,0,1:T(8,128)} %get-tuple-element.592, bf16[192,4,8,192]{3,2,0,1:T(8,128)(2,1)} %copy.114, pred[]{:T(512)S(6)} %compare.6, bf16[192,4,128]{2,0,1:T(8,128)(2,1)S(1)} %copy.122), kind=kOutput, calls=%fused_computation.7.clone.1 | convolution fusion | flops 304349184 | bytes 8847361 | tf_op jit(solution)/shard_map/while/body/eval_jaxpr/tngs,snd->tngd/dot_general | solution.py:41
  391.2 3.6 fusion.105
  394.8 4.0 copy.114
  398.7 5.6 %bitcast_add_fusion.3 = f32[192,4,8,128]{3,2,0,1:T(8,128)} fusion(f32[192,4,8,128]{3,2,0,1:T(8,128)} %get-tuple-element.592, bf16[192,4,8,192]{3,2,0,1:T(8,128)(2,1)} %copy.114, pred[]{:T(512)S(6)} %compare.6, bf16[192,4,128]{2,0,1:T(8,128)(2,1)S(1)} %copy.122), kind=kOutput, calls=%fused_computation.7.clone.1 | convolution fusion | flops 304349184 | bytes 8847361 | tf_op jit(solution)/shard_map/while/body/eval_jaxpr/tngs,snd->tngd/dot_general | solution.py:41
  421.1 4.0 copy.114
  425.1 5.6 %bitcast_add_fusion.3 = f32[192,4,8,128]{3,2,0,1:T(8,128)} fusion(f32[192,4,8,128]{3,2,0,1:T(8,128)} %get-tuple-element.592, bf16[192,4,8,192]{3,2,0,1:T(8,128)(2,1)} %copy.114, pred[]{:T(512)S(6)} %compare.6, bf16[192,4,128]{2,0,1:T(8,128)(2,1)S(1)} %copy.122), kind=kOutput, calls=%fused_computation.7.clone.1 | convolution fusion | flops 304349184 | bytes 8847361 | tf_op jit(solution)/shard_map/while/body/eval_jaxpr/tngs,snd->tngd/dot_general | solution.py:41
  433.5 4.7 fusion.27
  438.2 3.8 fusion.44
  447.7 3.7 all-to-all-start.1
  452.1 5.2 %fusion.45 = bf16[192,4,128]{2,0,1:T(8,128)(2,1)S(1)} fusion(f32[192,4,128]{2,0,1:T(8,128)} %get-tuple-element.363, f32[4,192,192,8]{2,1,3,0:T(8,128)} %copy-done.8, f32[192,4,8]{0,2,1:T(8,128)S(1)} %copy-done.17, pred[192,192]{0,1:T(8,128)(4,1)S(1)} %copy-done.12, bf16[192,4,8,128]{3,2,1,0:T(8,128)(2,1)S(1)} %bitcast.207), kind=kOutput, calls=%fused_computation.52 | convolution fusion | flops 306905088 | bytes 6942720 | tf_op jit(solution)/shard_map/tngs,tngd->snd/dot_general | solution.py:48
  460.7 9.5 %all-to-all-done.1 = bf16[2,96,4096]{2,1,0:T(8,128)(2,1)S(1)} async-done(((bf16[2,96,4096]{2,1,0:T(8,128)(2,1)}), bf16[2,96,4096]{2,1,0:T(8,128)(2,1)S(1)}, u32[]{:S(2)}, u32[]{:S(2)}) %all-to-all-start.1) | async-done | bytes 1572896 | tf_op jit(solution)/shard_map/all_to_all | solution.py:102
  (465 shorter events, 252.2 us)
Async XLA Ops:
  3.4 22.3 %all-to-all-start = ((bf16[96,2,4096]{2,0,1:T(8,128)(2,1)}), bf16[96,2,4096]{2,0,1:T(8,128)(2,1)S(1)}, u32[]{:S(2)}, u32[]{:S(2)}) async-start(bf16[96,2,4096]{2,0,1:T(8,128)(2,1)} %bitcast.171), calls=%async_computation | async-start | bytes 3145728 | tf_op jit(solution)/shard_map/all_to_all | solution.py:53
  34.1 25.1 %collective-permute-start.1 = (bf16[192,4,128]{2,0,1:T(8,128)(2,1)}, bf16[192,4,128]{2,0,1:T(8,128)(2,1)}, u32[]{:S(2)}, u32[]{:S(2)}) collective-permute-start(bf16[192,4,128]{2,0,1:T(8,128)(2,1)} %copy.123), channel_id=1, source_target_pairs={{30,0},{0,2},{2,4},{4,6},{6,8},{8,10},{10,12},{12,14},{14,16},{16,... | collective-permute-start | bytes 589832 | tf_op jit(solution)/shard_map/while/body/eval_jaxpr/ppermute | solution.py:14
  37.7 21.5 %collective-permute-start = (bf16[192,4,128]{2,0,1:T(8,128)(2,1)S(1)}, bf16[192,4,128]{2,0,1:T(8,128)(2,1)}, u32[]{:S(2)}, u32[]{:S(2)}) collective-permute-start(bf16[192,4,128]{2,0,1:T(8,128)(2,1)S(1)} %copy.122), channel_id=1, source_target_pairs={{30,0},{0,2},{2,4},{4,6},{6,8},{8,10},{10,12},{12,14},{14,16},{16,... | collective-permute-start | bytes 589832 | tf_op jit(solution)/shard_map/while/body/eval_jaxpr/ppermute | solution.py:14
  45.3 13.9 %collective-permute-start.2 = (f32[192,4,128]{2,0,1:T(8,128)}, f32[192,4,128]{2,0,1:T(8,128)}, u32[]{:S(2)}, u32[]{:S(2)}) collective-permute-start(f32[192,4,128]{2,0,1:T(8,128)} %fusion.104), channel_id=1, source_target_pairs={{30,0},{0,2},{2,4},{4,6},{6,8},{8,10},{10,12},{12,14},{14,16},{16,... | collective-permute-start | bytes 1179656 | tf_op jit(solution)/shard_map/while/body/eval_jaxpr/ppermute | solution.py:14
  61.1 25.0 %collective-permute-start.1 = (bf16[192,4,128]{2,0,1:T(8,128)(2,1)}, bf16[192,4,128]{2,0,1:T(8,128)(2,1)}, u32[]{:S(2)}, u32[]{:S(2)}) collective-permute-start(bf16[192,4,128]{2,0,1:T(8,128)(2,1)} %copy.123), channel_id=1, source_target_pairs={{30,0},{0,2},{2,4},{4,6},{6,8},{8,10},{10,12},{12,14},{14,16},{16,... | collective-permute-start | bytes 589832 | tf_op jit(solution)/shard_map/while/body/eval_jaxpr/ppermute | solution.py:14
  63.6 22.5 %collective-permute-start = (bf16[192,4,128]{2,0,1:T(8,128)(2,1)S(1)}, bf16[192,4,128]{2,0,1:T(8,128)(2,1)}, u32[]{:S(2)}, u32[]{:S(2)}) collective-permute-start(bf16[192,4,128]{2,0,1:T(8,128)(2,1)S(1)} %copy.122), channel_id=1, source_target_pairs={{30,0},{0,2},{2,4},{4,6},{6,8},{8,10},{10,12},{12,14},{14,16},{16,... | collective-permute-start | bytes 589832 | tf_op jit(solution)/shard_map/while/body/eval_jaxpr/ppermute | solution.py:14
  71.2 14.9 %collective-permute-start.2 = (f32[192,4,128]{2,0,1:T(8,128)}, f32[192,4,128]{2,0,1:T(8,128)}, u32[]{:S(2)}, u32[]{:S(2)}) collective-permute-start(f32[192,4,128]{2,0,1:T(8,128)} %fusion.104), channel_id=1, source_target_pairs={{30,0},{0,2},{2,4},{4,6},{6,8},{8,10},{10,12},{12,14},{14,16},{16,... | collective-permute-start | bytes 1179656 | tf_op jit(solution)/shard_map/while/body/eval_jaxpr/ppermute | solution.py:14
  87.9 23.6 %collective-permute-start.1 = (bf16[192,4,128]{2,0,1:T(8,128)(2,1)}, bf16[192,4,128]{2,0,1:T(8,128)(2,1)}, u32[]{:S(2)}, u32[]{:S(2)}) collective-permute-start(bf16[192,4,128]{2,0,1:T(8,128)(2,1)} %copy.123), channel_id=1, source_target_pairs={{30,0},{0,2},{2,4},{4,6},{6,8},{8,10},{10,12},{12,14},{14,16},{16,... | collective-permute-start | bytes 589832 | tf_op jit(solution)/shard_map/while/body/eval_jaxpr/ppermute | solution.py:14
  90.4 21.1 %collective-permute-start = (bf16[192,4,128]{2,0,1:T(8,128)(2,1)S(1)}, bf16[192,4,128]{2,0,1:T(8,128)(2,1)}, u32[]{:S(2)}, u32[]{:S(2)}) collective-permute-start(bf16[192,4,128]{2,0,1:T(8,128)(2,1)S(1)} %copy.122), channel_id=1, source_target_pairs={{30,0},{0,2},{2,4},{4,6},{6,8},{8,10},{10,12},{12,14},{14,16},{16,... | collective-permute-start | bytes 589832 | tf_op jit(solution)/shard_map/while/body/eval_jaxpr/ppermute | solution.py:14
  98.0 13.5 %collective-permute-start.2 = (f32[192,4,128]{2,0,1:T(8,128)}, f32[192,4,128]{2,0,1:T(8,128)}, u32[]{:S(2)}, u32[]{:S(2)}) collective-permute-start(f32[192,4,128]{2,0,1:T(8,128)} %fusion.104), channel_id=1, source_target_pairs={{30,0},{0,2},{2,4},{4,6},{6,8},{8,10},{10,12},{12,14},{14,16},{16,... | collective-permute-start | bytes 1179656 | tf_op jit(solution)/shard_map/while/body/eval_jaxpr/ppermute | solution.py:14
  101.9 9.6 %collective-permute-start.3 = (f32[192,4,128]{2,0,1:T(8,128)}, f32[192,4,128]{2,0,1:T(8,128)}, u32[]{:S(2)}, u32[]{:S(2)}) collective-permute-start(f32[192,4,128]{2,0,1:T(8,128)} %fusion.105), channel_id=1, source_target_pairs={{30,0},{0,2},{2,4},{4,6},{6,8},{8,10},{10,12},{12,14},{14,16},{16,... | collective-permute-start | bytes 1179656 | tf_op jit(solution)/shard_map/while/body/eval_jaxpr/ppermute | solution.py:14
  113.4 25.4 %collective-permute-start.1 = (bf16[192,4,128]{2,0,1:T(8,128)(2,1)}, bf16[192,4,128]{2,0,1:T(8,128)(2,1)}, u32[]{:S(2)}, u32[]{:S(2)}) collective-permute-start(bf16[192,4,128]{2,0,1:T(8,128)(2,1)} %copy.123), channel_id=1, source_target_pairs={{30,0},{0,2},{2,4},{4,6},{6,8},{8,10},{10,12},{12,14},{14,16},{16,... | collective-permute-start | bytes 589832 | tf_op jit(solution)/shard_map/while/body/eval_jaxpr/ppermute | solution.py:14
  115.9 22.9 %collective-permute-start = (bf16[192,4,128]{2,0,1:T(8,128)(2,1)S(1)}, bf16[192,4,128]{2,0,1:T(8,128)(2,1)}, u32[]{:S(2)}, u32[]{:S(2)}) collective-permute-start(bf16[192,4,128]{2,0,1:T(8,128)(2,1)S(1)} %copy.122), channel_id=1, source_target_pairs={{30,0},{0,2},{2,4},{4,6},{6,8},{8,10},{10,12},{12,14},{14,16},{16,... | collective-permute-start | bytes 589832 | tf_op jit(solution)/shard_map/while/body/eval_jaxpr/ppermute | solution.py:14
  123.6 15.3 %collective-permute-start.2 = (f32[192,4,128]{2,0,1:T(8,128)}, f32[192,4,128]{2,0,1:T(8,128)}, u32[]{:S(2)}, u32[]{:S(2)}) collective-permute-start(f32[192,4,128]{2,0,1:T(8,128)} %fusion.104), channel_id=1, source_target_pairs={{30,0},{0,2},{2,4},{4,6},{6,8},{8,10},{10,12},{12,14},{14,16},{16,... | collective-permute-start | bytes 1179656 | tf_op jit(solution)/shard_map/while/body/eval_jaxpr/ppermute | solution.py:14
  140.8 24.5 %collective-permute-start.1 = (bf16[192,4,128]{2,0,1:T(8,128)(2,1)}, bf16[192,4,128]{2,0,1:T(8,128)(2,1)}, u32[]{:S(2)}, u32[]{:S(2)}) collective-permute-start(bf16[192,4,128]{2,0,1:T(8,128)(2,1)} %copy.123), channel_id=1, source_target_pairs={{30,0},{0,2},{2,4},{4,6},{6,8},{8,10},{10,12},{12,14},{14,16},{16,... | collective-permute-start | bytes 589832 | tf_op jit(solution)/shard_map/while/body/eval_jaxpr/ppermute | solution.py:14
  142.8 22.5 %collective-permute-start = (bf16[192,4,128]{2,0,1:T(8,128)(2,1)S(1)}, bf16[192,4,128]{2,0,1:T(8,128)(2,1)}, u32[]{:S(2)}, u32[]{:S(2)}) collective-permute-start(bf16[192,4,128]{2,0,1:T(8,128)(2,1)S(1)} %copy.122), channel_id=1, source_target_pairs={{30,0},{0,2},{2,4},{4,6},{6,8},{8,10},{10,12},{12,14},{14,16},{16,... | collective-permute-start | bytes 589832 | tf_op jit(solution)/shard_map/while/body/eval_jaxpr/ppermute | solution.py:14
  150.4 14.9 %collective-permute-start.2 = (f32[192,4,128]{2,0,1:T(8,128)}, f32[192,4,128]{2,0,1:T(8,128)}, u32[]{:S(2)}, u32[]{:S(2)}) collective-permute-start(f32[192,4,128]{2,0,1:T(8,128)} %fusion.104), channel_id=1, source_target_pairs={{30,0},{0,2},{2,4},{4,6},{6,8},{8,10},{10,12},{12,14},{14,16},{16,... | collective-permute-start | bytes 1179656 | tf_op jit(solution)/shard_map/while/body/eval_jaxpr/ppermute | solution.py:14
  167.2 25.0 %collective-permute-start.1 = (bf16[192,4,128]{2,0,1:T(8,128)(2,1)}, bf16[192,4,128]{2,0,1:T(8,128)(2,1)}, u32[]{:S(2)}, u32[]{:S(2)}) collective-permute-start(bf16[192,4,128]{2,0,1:T(8,128)(2,1)} %copy.123), channel_id=1, source_target_pairs={{30,0},{0,2},{2,4},{4,6},{6,8},{8,10},{10,12},{12,14},{14,16},{16,... | collective-permute-start | bytes 589832 | tf_op jit(solution)/shard_map/while/body/eval_jaxpr/ppermute | solution.py:14
  169.7 22.5 %collective-permute-start = (bf16[192,4,128]{2,0,1:T(8,128)(2,1)S(1)}, bf16[192,4,128]{2,0,1:T(8,128)(2,1)}, u32[]{:S(2)}, u32[]{:S(2)}) collective-permute-start(bf16[192,4,128]{2,0,1:T(8,128)(2,1)S(1)} %copy.122), channel_id=1, source_target_pairs={{30,0},{0,2},{2,4},{4,6},{6,8},{8,10},{10,12},{12,14},{14,16},{16,... | collective-permute-start | bytes 589832 | tf_op jit(solution)/shard_map/while/body/eval_jaxpr/ppermute | solution.py:14
  177.3 14.9 %collective-permute-start.2 = (f32[192,4,128]{2,0,1:T(8,128)}, f32[192,4,128]{2,0,1:T(8,128)}, u32[]{:S(2)}, u32[]{:S(2)}) collective-permute-start(f32[192,4,128]{2,0,1:T(8,128)} %fusion.104), channel_id=1, source_target_pairs={{30,0},{0,2},{2,4},{4,6},{6,8},{8,10},{10,12},{12,14},{14,16},{16,... | collective-permute-start | bytes 1179656 | tf_op jit(solution)/shard_map/while/body/eval_jaxpr/ppermute | solution.py:14
  194.0 24.5 %collective-permute-start.1 = (bf16[192,4,128]{2,0,1:T(8,128)(2,1)}, bf16[192,4,128]{2,0,1:T(8,128)(2,1)}, u32[]{:S(2)}, u32[]{:S(2)}) collective-permute-start(bf16[192,4,128]{2,0,1:T(8,128)(2,1)} %copy.123), channel_id=1, source_target_pairs={{30,0},{0,2},{2,4},{4,6},{6,8},{8,10},{10,12},{12,14},{14,16},{16,... | collective-permute-start | bytes 589832 | tf_op jit(solution)/shard_map/while/body/eval_jaxpr/ppermute | solution.py:14
  196.5 22.0 %collective-permute-start = (bf16[192,4,128]{2,0,1:T(8,128)(2,1)S(1)}, bf16[192,4,128]{2,0,1:T(8,128)(2,1)}, u32[]{:S(2)}, u32[]{:S(2)}) collective-permute-start(bf16[192,4,128]{2,0,1:T(8,128)(2,1)S(1)} %copy.122), channel_id=1, source_target_pairs={{30,0},{0,2},{2,4},{4,6},{6,8},{8,10},{10,12},{12,14},{14,16},{16,... | collective-permute-start | bytes 589832 | tf_op jit(solution)/shard_map/while/body/eval_jaxpr/ppermute | solution.py:14
  204.1 14.4 %collective-permute-start.2 = (f32[192,4,128]{2,0,1:T(8,128)}, f32[192,4,128]{2,0,1:T(8,128)}, u32[]{:S(2)}, u32[]{:S(2)}) collective-permute-start(f32[192,4,128]{2,0,1:T(8,128)} %fusion.104), channel_id=1, source_target_pairs={{30,0},{0,2},{2,4},{4,6},{6,8},{8,10},{10,12},{12,14},{14,16},{16,... | collective-permute-start | bytes 1179656 | tf_op jit(solution)/shard_map/while/body/eval_jaxpr/ppermute | solution.py:14
  220.4 24.6 %collective-permute-start.1 = (bf16[192,4,128]{2,0,1:T(8,128)(2,1)}, bf16[192,4,128]{2,0,1:T(8,128)(2,1)}, u32[]{:S(2)}, u32[]{:S(2)}) collective-permute-start(bf16[192,4,128]{2,0,1:T(8,128)(2,1)} %copy.123), channel_id=1, source_target_pairs={{30,0},{0,2},{2,4},{4,6},{6,8},{8,10},{10,12},{12,14},{14,16},{16,... | collective-permute-start | bytes 589832 | tf_op jit(solution)/shard_map/while/body/eval_jaxpr/ppermute | solution.py:14
  222.0 23.0 %collective-permute-start = (bf16[192,4,128]{2,0,1:T(8,128)(2,1)S(1)}, bf16[192,4,128]{2,0,1:T(8,128)(2,1)}, u32[]{:S(2)}, u32[]{:S(2)}) collective-permute-start(bf16[192,4,128]{2,0,1:T(8,128)(2,1)S(1)} %copy.122), channel_id=1, source_target_pairs={{30,0},{0,2},{2,4},{4,6},{6,8},{8,10},{10,12},{12,14},{14,16},{16,... | collective-permute-start | bytes 589832 | tf_op jit(solution)/shard_map/while/body/eval_jaxpr/ppermute | solution.py:14
  229.6 15.4 %collective-permute-start.2 = (f32[192,4,128]{2,0,1:T(8,128)}, f32[192,4,128]{2,0,1:T(8,128)}, u32[]{:S(2)}, u32[]{:S(2)}) collective-permute-start(f32[192,4,128]{2,0,1:T(8,128)} %fusion.104), channel_id=1, source_target_pairs={{30,0},{0,2},{2,4},{4,6},{6,8},{8,10},{10,12},{12,14},{14,16},{16,... | collective-permute-start | bytes 1179656 | tf_op jit(solution)/shard_map/while/body/eval_jaxpr/ppermute | solution.py:14
  246.9 24.5 %collective-permute-start.1 = (bf16[192,4,128]{2,0,1:T(8,128)(2,1)}, bf16[192,4,128]{2,0,1:T(8,128)(2,1)}, u32[]{:S(2)}, u32[]{:S(2)}) collective-permute-start(bf16[192,4,128]{2,0,1:T(8,128)(2,1)} %copy.123), channel_id=1, source_target_pairs={{30,0},{0,2},{2,4},{4,6},{6,8},{8,10},{10,12},{12,14},{14,16},{16,... | collective-permute-start | bytes 589832 | tf_op jit(solution)/shard_map/while/body/eval_jaxpr/ppermute | solution.py:14
  248.9 22.5 %collective-permute-start = (bf16[192,4,128]{2,0,1:T(8,128)(2,1)S(1)}, bf16[192,4,128]{2,0,1:T(8,128)(2,1)}, u32[]{:S(2)}, u32[]{:S(2)}) collective-permute-start(bf16[192,4,128]{2,0,1:T(8,128)(2,1)S(1)} %copy.122), channel_id=1, source_target_pairs={{30,0},{0,2},{2,4},{4,6},{6,8},{8,10},{10,12},{12,14},{14,16},{16,... | collective-permute-start | bytes 589832 | tf_op jit(solution)/shard_map/while/body/eval_jaxpr/ppermute | solution.py:14
  256.5 14.9 %collective-permute-start.2 = (f32[192,4,128]{2,0,1:T(8,128)}, f32[192,4,128]{2,0,1:T(8,128)}, u32[]{:S(2)}, u32[]{:S(2)}) collective-permute-start(f32[192,4,128]{2,0,1:T(8,128)} %fusion.104), channel_id=1, source_target_pairs={{30,0},{0,2},{2,4},{4,6},{6,8},{8,10},{10,12},{12,14},{14,16},{16,... | collective-permute-start | bytes 1179656 | tf_op jit(solution)/shard_map/while/body/eval_jaxpr/ppermute | solution.py:14
  273.3 25.0 %collective-permute-start.1 = (bf16[192,4,128]{2,0,1:T(8,128)(2,1)}, bf16[192,4,128]{2,0,1:T(8,128)(2,1)}, u32[]{:S(2)}, u32[]{:S(2)}) collective-permute-start(bf16[192,4,128]{2,0,1:T(8,128)(2,1)} %copy.123), channel_id=1, source_target_pairs={{30,0},{0,2},{2,4},{4,6},{6,8},{8,10},{10,12},{12,14},{14,16},{16,... | collective-permute-start | bytes 589832 | tf_op jit(solution)/shard_map/while/body/eval_jaxpr/ppermute | solution.py:14
  275.8 22.5 %collective-permute-start = (bf16[192,4,128]{2,0,1:T(8,128)(2,1)S(1)}, bf16[192,4,128]{2,0,1:T(8,128)(2,1)}, u32[]{:S(2)}, u32[]{:S(2)}) collective-permute-start(bf16[192,4,128]{2,0,1:T(8,128)(2,1)S(1)} %copy.122), channel_id=1, source_target_pairs={{30,0},{0,2},{2,4},{4,6},{6,8},{8,10},{10,12},{12,14},{14,16},{16,... | collective-permute-start | bytes 589832 | tf_op jit(solution)/shard_map/while/body/eval_jaxpr/ppermute | solution.py:14
  283.3 14.9 %collective-permute-start.2 = (f32[192,4,128]{2,0,1:T(8,128)}, f32[192,4,128]{2,0,1:T(8,128)}, u32[]{:S(2)}, u32[]{:S(2)}) collective-permute-start(f32[192,4,128]{2,0,1:T(8,128)} %fusion.104), channel_id=1, source_target_pairs={{30,0},{0,2},{2,4},{4,6},{6,8},{8,10},{10,12},{12,14},{14,16},{16,... | collective-permute-start | bytes 1179656 | tf_op jit(solution)/shard_map/while/body/eval_jaxpr/ppermute | solution.py:14
  300.1 24.5 %collective-permute-start.1 = (bf16[192,4,128]{2,0,1:T(8,128)(2,1)}, bf16[192,4,128]{2,0,1:T(8,128)(2,1)}, u32[]{:S(2)}, u32[]{:S(2)}) collective-permute-start(bf16[192,4,128]{2,0,1:T(8,128)(2,1)} %copy.123), channel_id=1, source_target_pairs={{30,0},{0,2},{2,4},{4,6},{6,8},{8,10},{10,12},{12,14},{14,16},{16,... | collective-permute-start | bytes 589832 | tf_op jit(solution)/shard_map/while/body/eval_jaxpr/ppermute | solution.py:14
  302.6 22.0 %collective-permute-start = (bf16[192,4,128]{2,0,1:T(8,128)(2,1)S(1)}, bf16[192,4,128]{2,0,1:T(8,128)(2,1)}, u32[]{:S(2)}, u32[]{:S(2)}) collective-permute-start(bf16[192,4,128]{2,0,1:T(8,128)(2,1)S(1)} %copy.122), channel_id=1, source_target_pairs={{30,0},{0,2},{2,4},{4,6},{6,8},{8,10},{10,12},{12,14},{14,16},{16,... | collective-permute-start | bytes 589832 | tf_op jit(solution)/shard_map/while/body/eval_jaxpr/ppermute | solution.py:14
  310.2 14.4 %collective-permute-start.2 = (f32[192,4,128]{2,0,1:T(8,128)}, f32[192,4,128]{2,0,1:T(8,128)}, u32[]{:S(2)}, u32[]{:S(2)}) collective-permute-start(f32[192,4,128]{2,0,1:T(8,128)} %fusion.104), channel_id=1, source_target_pairs={{30,0},{0,2},{2,4},{4,6},{6,8},{8,10},{10,12},{12,14},{14,16},{16,... | collective-permute-start | bytes 1179656 | tf_op jit(solution)/shard_map/while/body/eval_jaxpr/ppermute | solution.py:14
  326.5 24.6 %collective-permute-start.1 = (bf16[192,4,128]{2,0,1:T(8,128)(2,1)}, bf16[192,4,128]{2,0,1:T(8,128)(2,1)}, u32[]{:S(2)}, u32[]{:S(2)}) collective-permute-start(bf16[192,4,128]{2,0,1:T(8,128)(2,1)} %copy.123), channel_id=1, source_target_pairs={{30,0},{0,2},{2,4},{4,6},{6,8},{8,10},{10,12},{12,14},{14,16},{16,... | collective-permute-start | bytes 589832 | tf_op jit(solution)/shard_map/while/body/eval_jaxpr/ppermute | solution.py:14
  328.1 23.0 %collective-permute-start = (bf16[192,4,128]{2,0,1:T(8,128)(2,1)S(1)}, bf16[192,4,128]{2,0,1:T(8,128)(2,1)}, u32[]{:S(2)}, u32[]{:S(2)}) collective-permute-start(bf16[192,4,128]{2,0,1:T(8,128)(2,1)S(1)} %copy.122), channel_id=1, source_target_pairs={{30,0},{0,2},{2,4},{4,6},{6,8},{8,10},{10,12},{12,14},{14,16},{16,... | collective-permute-start | bytes 589832 | tf_op jit(solution)/shard_map/while/body/eval_jaxpr/ppermute | solution.py:14
  335.7 15.4 %collective-permute-start.2 = (f32[192,4,128]{2,0,1:T(8,128)}, f32[192,4,128]{2,0,1:T(8,128)}, u32[]{:S(2)}, u32[]{:S(2)}) collective-permute-start(f32[192,4,128]{2,0,1:T(8,128)} %fusion.104), channel_id=1, source_target_pairs={{30,0},{0,2},{2,4},{4,6},{6,8},{8,10},{10,12},{12,14},{14,16},{16,... | collective-permute-start | bytes 1179656 | tf_op jit(solution)/shard_map/while/body/eval_jaxpr/ppermute | solution.py:14
  353.0 24.5 %collective-permute-start.1 = (bf16[192,4,128]{2,0,1:T(8,128)(2,1)}, bf16[192,4,128]{2,0,1:T(8,128)(2,1)}, u32[]{:S(2)}, u32[]{:S(2)}) collective-permute-start(bf16[192,4,128]{2,0,1:T(8,128)(2,1)} %copy.123), channel_id=1, source_target_pairs={{30,0},{0,2},{2,4},{4,6},{6,8},{8,10},{10,12},{12,14},{14,16},{16,... | collective-permute-start | bytes 589832 | tf_op jit(solution)/shard_map/while/body/eval_jaxpr/ppermute | solution.py:14
  355.0 22.6 %collective-permute-start = (bf16[192,4,128]{2,0,1:T(8,128)(2,1)S(1)}, bf16[192,4,128]{2,0,1:T(8,128)(2,1)}, u32[]{:S(2)}, u32[]{:S(2)}) collective-permute-start(bf16[192,4,128]{2,0,1:T(8,128)(2,1)S(1)} %copy.122), channel_id=1, source_target_pairs={{30,0},{0,2},{2,4},{4,6},{6,8},{8,10},{10,12},{12,14},{14,16},{16,... | collective-permute-start | bytes 589832 | tf_op jit(solution)/shard_map/while/body/eval_jaxpr/ppermute | solution.py:14
  362.6 15.0 %collective-permute-start.2 = (f32[192,4,128]{2,0,1:T(8,128)}, f32[192,4,128]{2,0,1:T(8,128)}, u32[]{:S(2)}, u32[]{:S(2)}) collective-permute-start(f32[192,4,128]{2,0,1:T(8,128)} %fusion.104), channel_id=1, source_target_pairs={{30,0},{0,2},{2,4},{4,6},{6,8},{8,10},{10,12},{12,14},{14,16},{16,... | collective-permute-start | bytes 1179656 | tf_op jit(solution)/shard_map/while/body/eval_jaxpr/ppermute | solution.py:14
  379.4 25.0 %collective-permute-start.1 = (bf16[192,4,128]{2,0,1:T(8,128)(2,1)}, bf16[192,4,128]{2,0,1:T(8,128)(2,1)}, u32[]{:S(2)}, u32[]{:S(2)}) collective-permute-start(bf16[192,4,128]{2,0,1:T(8,128)(2,1)} %copy.123), channel_id=1, source_target_pairs={{30,0},{0,2},{2,4},{4,6},{6,8},{8,10},{10,12},{12,14},{14,16},{16,... | collective-permute-start | bytes 589832 | tf_op jit(solution)/shard_map/while/body/eval_jaxpr/ppermute | solution.py:14
  381.8 22.5 %collective-permute-start = (bf16[192,4,128]{2,0,1:T(8,128)(2,1)S(1)}, bf16[192,4,128]{2,0,1:T(8,128)(2,1)}, u32[]{:S(2)}, u32[]{:S(2)}) collective-permute-start(bf16[192,4,128]{2,0,1:T(8,128)(2,1)S(1)} %copy.122), channel_id=1, source_target_pairs={{30,0},{0,2},{2,4},{4,6},{6,8},{8,10},{10,12},{12,14},{14,16},{16,... | collective-permute-start | bytes 589832 | tf_op jit(solution)/shard_map/while/body/eval_jaxpr/ppermute | solution.py:14
  389.4 14.9 %collective-permute-start.2 = (f32[192,4,128]{2,0,1:T(8,128)}, f32[192,4,128]{2,0,1:T(8,128)}, u32[]{:S(2)}, u32[]{:S(2)}) collective-permute-start(f32[192,4,128]{2,0,1:T(8,128)} %fusion.104), channel_id=1, source_target_pairs={{30,0},{0,2},{2,4},{4,6},{6,8},{8,10},{10,12},{12,14},{14,16},{16,... | collective-permute-start | bytes 1179656 | tf_op jit(solution)/shard_map/while/body/eval_jaxpr/ppermute | solution.py:14
  406.3 24.5 %collective-permute-start.1 = (bf16[192,4,128]{2,0,1:T(8,128)(2,1)}, bf16[192,4,128]{2,0,1:T(8,128)(2,1)}, u32[]{:S(2)}, u32[]{:S(2)}) collective-permute-start(bf16[192,4,128]{2,0,1:T(8,128)(2,1)} %copy.123), channel_id=1, source_target_pairs={{30,0},{0,2},{2,4},{4,6},{6,8},{8,10},{10,12},{12,14},{14,16},{16,... | collective-permute-start | bytes 589832 | tf_op jit(solution)/shard_map/while/body/eval_jaxpr/ppermute | solution.py:14
  408.7 22.0 %collective-permute-start = (bf16[192,4,128]{2,0,1:T(8,128)(2,1)S(1)}, bf16[192,4,128]{2,0,1:T(8,128)(2,1)}, u32[]{:S(2)}, u32[]{:S(2)}) collective-permute-start(bf16[192,4,128]{2,0,1:T(8,128)(2,1)S(1)} %copy.122), channel_id=1, source_target_pairs={{30,0},{0,2},{2,4},{4,6},{6,8},{8,10},{10,12},{12,14},{14,16},{16,... | collective-permute-start | bytes 589832 | tf_op jit(solution)/shard_map/while/body/eval_jaxpr/ppermute | solution.py:14
  416.3 14.4 %collective-permute-start.2 = (f32[192,4,128]{2,0,1:T(8,128)}, f32[192,4,128]{2,0,1:T(8,128)}, u32[]{:S(2)}, u32[]{:S(2)}) collective-permute-start(f32[192,4,128]{2,0,1:T(8,128)} %fusion.104), channel_id=1, source_target_pairs={{30,0},{0,2},{2,4},{4,6},{6,8},{8,10},{10,12},{12,14},{14,16},{16,... | collective-permute-start | bytes 1179656 | tf_op jit(solution)/shard_map/while/body/eval_jaxpr/ppermute | solution.py:14
  447.7 22.5 %all-to-all-start.1 = ((bf16[2,96,4096]{2,1,0:T(8,128)(2,1)}), bf16[2,96,4096]{2,1,0:T(8,128)(2,1)S(1)}, u32[]{:S(2)}, u32[]{:S(2)}) async-start(bf16[2,96,4096]{2,1,0:T(8,128)(2,1)} %convert_element_type.65), calls=%async_computation.1 | async-start | bytes 3145728 | tf_op jit(solution)/shard_map/all_to_all | solution.py:102
  (104 other events, 424.7 us)
where the time goes:
time: 477 us; the launch traced here: 471 us
  matrix products  262 us (55%)
  local copies, waits for them, and re-layouts  126 us (26%)
  starting transfers between devices  53.8 us (11%)
  waiting for transfers between devices  19 us (4%)
  other arithmetic  8.88 us (2%)
    dot_general x16, matrix products, attend_block(): jnp.einsum('tngs,snd->tngd', dscores, key_block, preferred_element_type=j...  86.5 us
    convert_element_type x15, local copies, waits for them, and re-layouts, attend_block(): dscores = (prob_full * (dprobs - row_delta[..., None])).astype(jnp.bfloat16)  59.4 us
    dot_general x16, matrix products, attend_block(): jnp.einsum('tngs,tngd->snd', prob_low, grad_heads, preferred_element_type...  58.7 us
    dot_general x16, matrix products, attend_block(): jnp.einsum('tngd,snd->tngs', grad_heads, value_block, preferred_element_t...  49.7 us
    dot_general x16, matrix products, attend_block(): jnp.einsum('tngs,tngd->snd', dscores, query_heads, preferred_element_type...  49.5 us
    ppermute x62, starting transfers between devices, passed_along(): return lax.ppermute(block, axis, route)  46.4 us
    while x180, local copies, waits for them, and re-layouts  45.6 us
    dot_general x16, matrix products, attend_block(): jnp.einsum('tngd,snd->tngs', query_heads, key_block, preferred_element_ty...  17.6 us
  transfers between devices with their start and end apart: 64, of which 3 were waited for; matrix products, arithmetic and copies ran while one was open for 72% of the time, Pallas kernels for 0%

commit v1 on v0

v1 whole, which is shorter than its diff:
```python
import functools
import math

import jax
import jax.numpy as jnp
from jax import lax
from jax.experimental import pallas as pl
from jax.experimental.pallas import tpu as pltpu
from jax.sharding import PartitionSpec as P

QH = 64
KVH = 8
HD = 128
GROUPS = QH // KVH
KEYS = 256
LOG2E = math.log2(math.e)


def attend_kernel(
    slot_of_ref, my_span_ref,
    q_ref, d_ref, k_ref, v_ref, lse_ref, delta_ref, base_ref,
    dq_ref, dk_ref, dv_ref,
    ks, kt, vs, qs, qt, ds_rows, dt, dqt, dk_acc, dv_acc,
):
    span = base_ref.shape[1] // GROUPS
    seq = k_ref.shape[0]
    slots = q_ref.shape[0] // span
    inv_root = HD ** -0.5

    def place(p, _):
        src = pl.ds(pl.multiple_of(slot_of_ref[p] * span, span), span)
        dst = pl.ds(pl.multiple_of(p * span, span), span)
        ks[dst, :] = k_ref[src, :]
        vs[dst, :] = v_ref[src, :]
        return 0

    lax.fori_loop(0, seq // span, place, 0)

    def turn(c, _):
        rows = pl.ds(pl.multiple_of(c * KEYS, KEYS), KEYS)
        kt[c] = ks[rows, :].T
        dk_acc[rows, :] = jnp.zeros((KEYS, HD), jnp.float32)
        dv_acc[rows, :] = jnp.zeros((KEYS, HD), jnp.float32)
        return 0

    lax.fori_loop(0, seq // KEYS, turn, 0)

    def one_slot(s, _):
        rows = pl.ds(pl.multiple_of(s * span, span), span)
        for g in range(GROUPS):
            part = slice(g * span, (g + 1) * span)
            cols = slice(g * HD, (g + 1) * HD)
            qs[part, :] = q_ref[rows, cols]
            ds_rows[part, :] = d_ref[rows, cols]
        qt[...] = qs[...].T
        dt[...] = ds_rows[...].T
        dqt[...] = jnp.zeros_like(dqt)
        my_span = my_span_ref[s]

        def block(c, masked):
            keys = pl.ds(pl.multiple_of(c * KEYS, KEYS), KEYS)
            scores = jnp.dot(ks[keys, :], qt[...], preferred_element_type=jnp.float32)
            prob = jnp.exp2(scores * (inv_root * LOG2E) - lse_ref[0, s])
            if masked:
                key_pos = c * KEYS + lax.broadcasted_iota(jnp.int32, prob.shape, 0)
                prob = jnp.where(my_span * span + base_ref[...] >= key_pos, prob, 0.0)
            dprob = jnp.dot(vs[keys, :], dt[...], preferred_element_type=jnp.float32)
            dscore = (prob * (dprob - delta_ref[0, s])).astype(jnp.bfloat16)
            dv_acc[keys, :] += jnp.dot(
                prob.astype(jnp.bfloat16), ds_rows[...], preferred_element_type=jnp.float32
            )
            dk_acc[keys, :] += jnp.dot(dscore, qs[...], preferred_element_type=jnp.float32)
            dqt[...] += jnp.dot(kt[c], dscore, preferred_element_type=jnp.float32)

        whole = (my_span * span) // KEYS
        last = (my_span * span + span + KEYS - 1) // KEYS
        lax.fori_loop(0, whole, lambda c, _: (block(c, False), 0)[1], 0)
        lax.fori_loop(whole, last, lambda c, _: (block(c, True), 0)[1], 0)

        dq = (dqt[...].T * inv_root).astype(jnp.bfloat16)
        for g in range(GROUPS):
            dq_ref[rows, g * HD:(g + 1) * HD] = dq[g * span:(g + 1) * span, :]
        return 0

    lax.fori_loop(0, slots, one_slot, 0)

    def back(p, _):
        dst = pl.ds(pl.multiple_of(slot_of_ref[p] * span, span), span)
        src = pl.ds(pl.multiple_of(p * span, span), span)
        dk_ref[dst, :] = (dk_acc[src, :] * inv_root).astype(dk_ref.dtype)
        dv_ref[dst, :] = dv_acc[src, :].astype(dv_ref.dtype)
        return 0

    lax.fori_loop(0, seq // span, back, 0)


def attend(slot_of, my_spans, q, d, k, v, lse, delta, span, part_type):
    rows = q.shape[0]
    seq = k.shape[0]
    kv_heads = k.shape[1] // HD
    slots = rows // span
    wide = GROUPS * span
    base = jnp.tile(jnp.arange(span, dtype=jnp.int32), GROUPS)[None, :]
    pairs = kv_heads * wide * seq * slots

    def by_head(height, width):
        return pl.BlockSpec((height, width), lambda h, *_: (0, h))

    row_terms = pl.BlockSpec((1, slots, 1, wide), lambda h, *_: (h, 0, 0, 0))
    return pl.pallas_call(
        attend_kernel,
        grid_spec=pltpu.PrefetchScalarGridSpec(
            num_scalar_prefetch=2,
            grid=(kv_heads,),
            in_specs=[
                by_head(rows, GROUPS * HD), by_head(rows, GROUPS * HD),
                by_head(seq, HD), by_head(seq, HD),
                row_terms, row_terms,
                pl.BlockSpec((1, wide), lambda h, *_: (0, 0)),
            ],
            out_specs=[by_head(rows, GROUPS * HD), by_head(seq, HD), by_head(seq, HD)],
            scratch_shapes=[
                pltpu.VMEM((seq, HD), jnp.bfloat16),
                pltpu.VMEM((seq // KEYS, HD, KEYS), jnp.bfloat16),
                pltpu.VMEM((seq, HD), jnp.bfloat16),
                pltpu.VMEM((wide, HD), jnp.bfloat16),
                pltpu.VMEM((HD, wide), jnp.bfloat16),
                pltpu.VMEM((wide, HD), jnp.bfloat16),
                pltpu.VMEM((HD, wide), jnp.bfloat16),
                pltpu.VMEM((HD, wide), jnp.float32),
                pltpu.VMEM((seq, HD), jnp.float32),
                pltpu.VMEM((seq, HD), jnp.float32),
            ],
        ),
        out_shape=[
            jax.ShapeDtypeStruct(q.shape, jnp.bfloat16),
            jax.ShapeDtypeStruct(k.shape, part_type),
            jax.ShapeDtypeStruct(k.shape, part_type),
        ],
        compiler_params=pltpu.CompilerParams(vmem_limit_bytes=48 * 2**20),
        cost_estimate=pl.CostEstimate(
            flops=7 * pairs * HD, bytes_accessed=2**24, transcendentals=pairs // 2
        ),
        name="attend",
    )(slot_of, my_spans, q, d, k, v, lse, delta, base)


def row_terms_of(terms, kv_heads, span):
    rows = terms.shape[1]
    cut = terms.reshape(kv_heads, GROUPS, rows // span, span)
    return cut.transpose(0, 2, 1, 3).reshape(kv_heads, rows // span, 1, GROUPS * span)


def per_device(query_rows, key_rows, value_rows, attn_output, log_norms, grad_output, span_order):
    own_rows = query_rows.shape[0]
    span = own_rows // 2
    ctx = lax.axis_size("ctx")
    me = lax.axis_index("ctx")
    cores = 2 if (key_rows.shape[1] // HD) % 2 == 0 and ctx % 2 == 0 else 1
    chip_groups = [[i * cores + c for c in range(cores)] for i in range(ctx // cores)]
    ring_groups = [[i * cores + c for i in range(ctx // cores)] for c in range(cores)]

    def to_heads(x, split=1, concat=0):
        if cores == 1:
            return x
        return lax.all_to_all(
            x, "ctx", split_axis=split, concat_axis=concat, axis_index_groups=chip_groups, tiled=True
        )

    q = to_heads(query_rows)
    o = to_heads(attn_output)
    lse = to_heads(log_norms, 0, 1)
    d = to_heads(lax.all_to_all(grad_output, "head", split_axis=1, concat_axis=0, tiled=True))
    kv = jnp.concatenate([to_heads(key_rows), to_heads(value_rows)], axis=1)
    kv = lax.all_gather(kv, "ctx", axis=0, axis_index_groups=ring_groups, tiled=True)
    half = kv.shape[1] // 2
    kv_heads = half // HD
    rows = q.shape[0]
    delta = jnp.sum(
        (d.astype(jnp.float32) * o.astype(jnp.float32)).reshape(rows, kv_heads * GROUPS, HD), axis=-1
    ).T
    spans = span_order.shape[0]
    slots = rows // span
    slot_of = jnp.argsort(span_order).astype(jnp.int32)
    my_spans = lax.dynamic_slice_in_dim(span_order, (me // cores) * slots, slots)
    dq, dk, dv = attend(
        slot_of, my_spans, q, d, kv[:, :half], kv[:, half:],
        row_terms_of(lse * LOG2E, kv_heads, span), row_terms_of(delta, kv_heads, span),
        span, jnp.float32,
    )
    dkv = jnp.concatenate([dk, dv], axis=1)
    dkv = lax.psum_scatter(dkv, "ctx", scatter_dimension=0, axis_index_groups=ring_groups, tiled=True)
    dkv = dkv.astype(jnp.bfloat16)
    grad_key = to_heads(dkv[:, :half], 0, 1)
    grad_value = to_heads(dkv[:, half:], 0, 1)
    dq = to_heads(dq, 0, 1)
    grad_query = lax.all_to_all(dq, "head", split_axis=0, concat_axis=1, tiled=True)
    return (grad_query, grad_key, grad_value)


def solution(mesh):
    return jax.shard_map(
        per_device,
        mesh=mesh,
        in_specs=(
            P("ctx", "head"),
            P("ctx", "head"),
            P("ctx", "head"),
            P("ctx", "head"),
            P("head", "ctx"),
            P(("ctx", "head"), None),
            P(),
        ),
        out_specs=(P(("ctx", "head"), None), P("ctx", "head"), P("ctx", "head")),
        check_vma=False,
    )
```

time: 477 us -> 280 us (0.59)
  matrix products: 262 us -> 0 us
  local copies, waits for them, and re-layouts: 126 us -> 26.4 us
  waiting for transfers between devices: 19 us -> 103 us
  Pallas kernels: 0 us -> 49.9 us
  blocking collectives: 0 us -> 44.9 us
  starting transfers between devices: 53.8 us -> 21.3 us
  between operations: 0.9 us -> 14.2 us
  other arithmetic: 8.88 us -> 14.7 us
    dot_general x80 -> x0, matrix products: 262 us -> none  [the longest x16 86.5 us: attend_block(): jnp.einsum('tngs,snd->tngd', dscores, key_block, preferred_element_type=j...]
    reduce_scatter x0 -> x1, waiting for transfers between devices: none -> 83.1 us  [per_device(): lax.psum_scatter(dkv, 'ctx', scatter_dimension=0, axis_index_groups=ring_...]
    convert_element_type x19 -> x0, local copies, waits for them, and re-layouts: 63.9 us -> none  [the longest x15 59.4 us: attend_block(): dscores = (prob_full * (dprobs - row_delta[..., None])).astype(jnp.bfloat16)]
    pallas_call x0 -> x1, Pallas kernels: none -> 49.9 us  [attend(): pl.pallas_call(attend_kernel, grid_spec=pltpu.PrefetchScalarGridSpec(num_...]
    ppermute x62 -> x0, starting transfers between devices: 46.4 us -> none  [passed_along(): return lax.ppermute(block, axis, route)]
    while x180 -> x0, local copies, waits for them, and re-layouts: 45.6 us -> none
    all_to_all x0 -> x6, blocking collectives: none -> 44.9 us  [the longest x5 23.3 us: to_heads(): lax.all_to_all(x, 'ctx', split_axis=split, concat_axis=concat, axis_index...]
    all_to_all x1 -> x11, local copies, waits for them, and re-layouts: 1.25 us -> 15 us  [the longest x9 12.6 us: to_heads(): lax.all_to_all(x, 'ctx', split_axis=split, concat_axis=concat, axis_index...]
  transfers between devices with their start and end apart: 64 -> 7, of which waited for: 3 -> 4; matrix products, arithmetic and copies ran while one was open for 72% -> 8% of each run, Pallas kernels for 0% -> 0%
where the time goes in v1:
time: 280 us; the launch traced here: 275 us
  waiting for transfers between devices  103 us (37%)
  Pallas kernels  49.9 us (18%)
  blocking collectives  44.9 us (16%)
  local copies, waits for them, and re-layouts  26.4 us (9%)
  starting transfers between devices  21.3 us (8%)
  other arithmetic  14.7 us (5%)
  between operations  14.2 us (5%)
    reduce_scatter x1, waiting for transfers between devices, per_device(): lax.psum_scatter(dkv, 'ctx', scatter_dimension=0, axis_index_groups=ring_...  83.1 us
    pallas_call x1, Pallas kernels, attend(): pl.pallas_call(attend_kernel, grid_spec=pltpu.PrefetchScalarGridSpec(num_...  49.9 us
    all_to_all x5, blocking collectives, to_heads(): lax.all_to_all(x, 'ctx', split_axis=split, concat_axis=concat, axis_index...  23.3 us
    all_to_all x1, blocking collectives, per_device(): lax.all_to_all(dq, 'head', split_axis=0, concat_axis=1, tiled=True)  21.5 us
    all_to_all x4, starting transfers between devices, to_heads(): lax.all_to_all(x, 'ctx', split_axis=split, concat_axis=concat, axis_index...  17.4 us
    all_to_all x1, waiting for transfers between devices, per_device(): lax.all_to_all(grad_output, 'head', split_axis=1, concat_axis=0, tiled=True)  14 us
    all_to_all x9, local copies, waits for them, and re-layouts, to_heads(): lax.all_to_all(x, 'ctx', split_axis=split, concat_axis=concat, axis_index...  12.6 us
    concatenate x1, other arithmetic, per_device(): dkv = jnp.concatenate([dk, dv], axis=1)  6.37 us
  transfers between devices with their start and end apart: 7, of which 4 were waited for; matrix products, arithmetic and copies ran while one was open for 8% of the time, Pallas kernels for 0%

profile of v1, /device:TPU:9, one launch (start us, length us, event | category | flops | bytes accessed | tf_op | source)
XLA Modules:
  0.0 274.6 jit_solution(14913319922723645558)
XLA Ops:
  7.2 1.7 copy.85
  8.9 4.1 %all-to-all-start.3 = ((bf16[192,2,256]{2,0,1:T(8,128)(2,1)}), bf16[192,2,256]{2,0,1:T(8,128)(2,1)S(1)}, u32[]{:S(2)}, u32[]{:S(2)}) async-start(bf16[192,2,256]{2,0,1:T(8,128)(2,1)} %bitcast.61), calls=%async_computation.3 | async-start | bytes 393216 | tf_op jit(solution)/shard_map/all_to_all | solution.py:166
  13.0 0.9 copy.84
  14.0 0.2 all-to-all-done.3
  14.2 3.9 %all_to_all.191 = bf16[192,2,256]{2,0,1:T(8,128)(2,1)S(1)} all-to-all(bf16[192,2,256]{2,0,1:T(8,128)(2,1)S(1)} %bitcast.76), channel_id=1, replica_groups={{0,2},{4,6},{8,10},{12,14},{16,18},{20,22},{24,26},{28,30},{1,3},{5,7},..., dimensions={1} | all-to-all | bytes 393216 | tf_op jit(solution)/shard_map/all_to_all | solution.py:166
  18.0 0.8 pad_maximum_fusion.1
  18.9 0.0 all-gather.2.cloned.1.call-update
  18.9 3.6 %all-to-all-start.5 = ((f32[2,16,192]{2,1,0:T(8,128)}), f32[2,16,192]{2,1,0:T(8,128)S(1)}, u32[]{:S(2)}, u32[]{:S(2)}) async-start(f32[2,16,192]{2,1,0:T(8,128)} %bitcast.9), calls=%async_computation.5 | async-start | bytes 65536 | tf_op jit(solution)/shard_map/all_to_all | solution.py:166
  22.5 1.3 copy.82
  23.8 3.8 %all-to-all-start.1 = ((bf16[96,2,4096]{2,0,1:T(8,128)(2,1)}), bf16[96,2,4096]{2,0,1:T(8,128)(2,1)S(1)}, u32[]{:S(2)}, u32[]{:S(2)}) async-start(bf16[96,2,4096]{2,0,1:T(8,128)(2,1)} %bitcast.58), calls=%async_computation.1 | async-start | bytes 3145728 | tf_op jit(solution)/shard_map/all_to_all | solution.py:173
  27.6 0.1 dynamic_slice.3.my_span_ref
  27.7 1.6 sort.17
  29.3 0.1 broadcast_in_dim_tile.3.base_ref
  29.4 0.1 mul.27
  29.6 0.1 reshape.60.lse_ref
  29.7 1.2 copy.83
  30.9 0.7 copy-done.4
  31.7 1.3 copy.81
  32.9 14.0 %all-to-all-done.1 = bf16[96,2,4096]{2,0,1:T(8,128)(2,1)S(1)} async-done(((bf16[96,2,4096]{2,0,1:T(8,128)(2,1)}), bf16[96,2,4096]{2,0,1:T(8,128)(2,1)S(1)}, u32[]{:S(2)}, u32[]{:S(2)}) %all-to-all-start.1) | async-done | bytes 1572896 | tf_op jit(solution)/shard_map/all_to_all | solution.py:173
  46.9 5.7 %all-to-all-start.6 = ((bf16[192,2,2048]{2,0,1:T(8,128)(2,1)}), bf16[192,2,2048]{2,0,1:T(8,128)(2,1)}, u32[]{:S(2)}, u32[]{:S(2)}) async-start(bf16[192,2,2048]{2,0,1:T(8,128)(2,1)} %bitcast.57), calls=%async_computation.6 | async-start | bytes 3145728 | tf_op jit(solution)/shard_map/all_to_all | solution.py:166
  52.6 2.4 all_to_all.149
  55.0 2.0 copy.55
  57.0 4.7 %all_to_all.192 = bf16[192,2,2048]{2,0,1:T(8,128)(2,1)S(1)} all-to-all(bf16[192,2,2048]{2,0,1:T(8,128)(2,1)S(1)} %copy.55), channel_id=1, replica_groups={{0,2},{4,6},{8,10},{12,14},{16,18},{20,22},{24,26},{28,30},{1,3},{5,7},..., dimensions={1} | all-to-all | bytes 3145728 | tf_op jit(solution)/shard_map/all_to_all | solution.py:166
  61.7 4.0 %all-to-all-start = ((bf16[192,2,2048]{2,0,1:T(8,128)(2,1)}), bf16[192,2,2048]{2,0,1:T(8,128)(2,1)S(1)}, u32[]{:S(2)}, u32[]{:S(2)}) async-start(bf16[192,2,2048]{2,0,1:T(8,128)(2,1)} %bitcast.68), calls=%async_computation | async-start | bytes 3145728 | tf_op jit(solution)/shard_map/all_to_all | solution.py:166
  65.7 2.0 bitcast_multiply_fusion
  67.7 2.3 copy.75
  70.0 2.8 %reduce_sum.9 = f32[384,16]{1,0:T(8,128)S(1)} reduce(f32[384,16,128]{2,1,0:T(8,128)} %bitcast.65, f32[]{:T(128)} %constant.28.clone.1), dimensions={2}, to_apply=%region_1.0 | reduce | flops 780288 | bytes 3170308 | tf_op jit(solution)/shard_map/reduce_sum | solution.py:179
  72.8 0.1 copy.61
  72.9 0.1 reshape.61
  73.0 0.1 reshape.62.delta_ref
  73.1 5.9 %all-gather.2.cloned.1.call-done = bf16[3072,512]{1,0:T(8,128)(2,1)} async-done(((bf16[384,512]{1,0:T(8,128)(2,1)}), bf16[3072,512]{1,0:T(8,128)(2,1)}) %all-gather.2.cloned.1.call-update) | async-done | bytes 3145744 | tf_op jit(solution)/shard_map/all_gather | solution.py:175
  79.0 3.8 %fusion = (bf16[3072,256]{1,0:T(8,128)(2,1)}, bf16[3072,256]{1,0:T(8,128)(2,1)}) fusion(bf16[3072,512]{1,0:T(8,128)(2,1)} %all-gather.2.cloned.1.call-done), kind=kLoop, calls=%fused_computation.9 | loop fusion | bytes 6291456 | tf_op jit(solution)/shard_map/slice | solution.py:187
  82.8 49.9 %attend.1 = (bf16[384,2048]{1,0:T(8,128)(2,1)S(1)}, f32[3072,256]{1,0:T(8,128)}, f32[3072,256]{1,0:T(8,128)}) custom-call(s32[32]{0:T(128)S(1)} %get-tuple-element.7.slot_of_ref, s32[4]{0:T(128)S(1)} %dynamic_slice.3.my_span_ref, bf16[384,2048]{1,0:T(8,128)(2,1)S(1)} %bitcast.63, bf16[384,2048]{1,0:T(8,128)(2,1)S(1)} %bitcast.62, ...), custom_call_target="tpu_custom_call" | custom-call | flops 16911433728 | bytes 16777216 | tf_op jit(solution)/shard_map/attend/pallas_call | solution.py:110
  132.8 1.1 copy-done
  133.9 6.4 %pad_maximum_fusion = f32[3072,512]{1,0:T(8,128)} fusion(f32[3072,256]{1,0:T(8,128)} %get-tuple-element.10, f32[3072,256]{1,0:T(8,128)} %get-tuple-element.9), kind=kLoop, calls=%fused_computation | loop fusion | flops 1572864 | bytes 12582912 | tf_op jit(solution)/shard_map/concatenate | solution.py:191
  140.3 0.0 reduce-scatter.2.cloned.1.call-update
  140.3 1.4 copy-done.1
  141.7 6.5 %all_to_all.193 = bf16[2,192,2048]{2,1,0:T(8,128)(2,1)S(1)} all-to-all(bf16[2,192,2048]{2,1,0:T(8,128)(2,1)S(1)} %bitcast.64), channel_id=1, replica_groups={{0,2},{4,6},{8,10},{12,14},{16,18},{20,22},{24,26},{28,30},{1,3},{5,7},..., dimensions={0} | all-to-all | bytes 3145728 | tf_op jit(solution)/shard_map/all_to_all | solution.py:166
  148.2 1.6 copy.63
  149.8 1.2 all_to_all.168
  151.0 21.5 %all_to_all.194 = bf16[2,96,4096]{2,1,0:T(8,128)(2,1)S(1)} all-to-all(bf16[2,96,4096]{2,1,0:T(8,128)(2,1)S(1)} %all_to_all.168), channel_id=1, replica_groups=mesh['ctx'=16,'head'=2] {'head'}, dimensions={0} | all-to-all | bytes 3145728 | tf_op jit(solution)/shard_map/all_to_all | solution.py:197
  172.6 1.2 copy.72
  173.8 83.1 %reduce-scatter.2.cloned.1.call-done = f32[384,512]{1,0:T(8,128)} async-done(((f32[3072,512]{1,0:T(8,128)}), f32[384,512]{1,0:T(8,128)}) %reduce-scatter.2.cloned.1.call-update) | async-done | bytes 786448 | tf_op jit(solution)/shard_map/reduce_scatter | solution.py:192
  256.9 1.2 convert_element_type.19
  258.1 4.4 %all_to_all.195 = bf16[2,192,256]{2,1,0:T(8,128)(2,1)S(1)} all-to-all(bf16[2,192,256]{2,1,0:T(8,128)(2,1)S(1)} %bitcast.81), channel_id=1, replica_groups={{0,2},{4,6},{8,10},{12,14},{16,18},{20,22},{24,26},{28,30},{1,3},{5,7},..., dimensions={0} | all-to-all | bytes 393216 | tf_op jit(solution)/shard_map/all_to_all | solution.py:166
  262.5 0.7 copy.73
  263.2 3.9 %all_to_all.196 = bf16[2,192,256]{2,1,0:T(8,128)(2,1)S(1)} all-to-all(bf16[2,192,256]{2,1,0:T(8,128)(2,1)S(1)} %bitcast.80), channel_id=1, replica_groups={{0,2},{4,6},{8,10},{12,14},{16,18},{20,22},{24,26},{28,30},{1,3},{5,7},..., dimensions={0} | all-to-all | bytes 393216 | tf_op jit(solution)/shard_map/all_to_all | solution.py:166
  267.1 0.7 copy.74
  (21 shorter events, 0.1 us)
Async XLA Ops:
  7.2 15.3 %copy-start.2 = (bf16[96,8192]{1,0:T(8,128)(2,1)S(1)}, bf16[96,8192]{1,0:T(8,128)(2,1)}, u32[]{:S(2)}) copy-start(bf16[96,8192]{1,0:T(8,128)(2,1)} %param.12) | copy-start | bytes 4718596
  8.9 5.3 %all-to-all-start.3 = ((bf16[192,2,256]{2,0,1:T(8,128)(2,1)}), bf16[192,2,256]{2,0,1:T(8,128)(2,1)S(1)}, u32[]{:S(2)}, u32[]{:S(2)}) async-start(bf16[192,2,256]{2,0,1:T(8,128)(2,1)} %bitcast.61), calls=%async_computation.3 | async-start | bytes 393216 | tf_op jit(solution)/shard_map/all_to_all | solution.py:166
  13.0 66.0 %all-gather.2.cloned.1.call-start = ((), (), s32[]{:S(2)}) async-start(), calls=%async_computation.12 | async-start | bytes 3538944 | tf_op jit(solution)/shard_map/all_gather | solution.py:175
  18.9 4.9 %all-to-all-start.5 = ((f32[2,16,192]{2,1,0:T(8,128)}), f32[2,16,192]{2,1,0:T(8,128)S(1)}, u32[]{:S(2)}, u32[]{:S(2)}) async-start(f32[2,16,192]{2,1,0:T(8,128)} %bitcast.9), calls=%async_computation.5 | async-start | bytes 65536 | tf_op jit(solution)/shard_map/all_to_all | solution.py:166
  23.8 3.8 %copy-start.5 = (s32[32]{0:T(128)S(1)}, s32[32]{0:T(128)}, u32[]{:S(2)}) copy-start(s32[32]{0:T(128)} %param.13) | copy-start | bytes 388
  23.8 5.9 %copy-start.3 = (bf16[192,4096]{1,0:T(8,128)(2,1)S(1)}, bf16[192,4096]{1,0:T(8,128)(2,1)}, u32[]{:S(2)}) copy-start(bf16[192,4096]{1,0:T(8,128)(2,1)} %param.7) | copy-start | bytes 4718596
  23.8 23.1 %all-to-all-start.1 = ((bf16[96,2,4096]{2,0,1:T(8,128)(2,1)}), bf16[96,2,4096]{2,0,1:T(8,128)(2,1)S(1)}, u32[]{:S(2)}, u32[]{:S(2)}) async-start(bf16[96,2,4096]{2,0,1:T(8,128)(2,1)} %bitcast.58), calls=%async_computation.1 | async-start | bytes 3145728 | tf_op jit(solution)/shard_map/all_to_all | solution.py:173
  29.7 2.0 copy-start.4
  46.9 10.1 %all-to-all-start.6 = ((bf16[192,2,2048]{2,0,1:T(8,128)(2,1)}), bf16[192,2,2048]{2,0,1:T(8,128)(2,1)}, u32[]{:S(2)}, u32[]{:S(2)}) async-start(bf16[192,2,2048]{2,0,1:T(8,128)(2,1)} %bitcast.57), calls=%async_computation.6 | async-start | bytes 3145728 | tf_op jit(solution)/shard_map/all_to_all | solution.py:166
  61.7 21.1 %all-to-all-start = ((bf16[192,2,2048]{2,0,1:T(8,128)(2,1)}), bf16[192,2,2048]{2,0,1:T(8,128)(2,1)S(1)}, u32[]{:S(2)}, u32[]{:S(2)}) async-start(bf16[192,2,2048]{2,0,1:T(8,128)(2,1)} %bitcast.68), calls=%async_computation | async-start | bytes 3145728 | tf_op jit(solution)/shard_map/all_to_all | solution.py:166
  65.7 191.2 %reduce-scatter.2.cloned.1.call-start = ((), (), s32[]{:S(2)}) async-start(), calls=%async_computation.13 | async-start | bytes 7077888 | tf_op jit(solution)/shard_map/reduce_scatter | solution.py:192
  132.8 1.1 copy-start
  140.3 1.4 copy-start.1
Sparse Core Ops, SparseCore 0:
  19.0 59.9 all-gather.1
  140.4 116.4 reduce-scatter.1

commit v2 on v1

--- a/solution.py
+++ b/solution.py
@@ -145,6 +145,376 @@
     )(slot_of, my_spans, q, d, k, v, lse, delta, base)
 
 
+MESH = pl.DeviceIdType.MESH
+NX = 2
+
+
+def place_of():
+    me = lax.axis_index("ctx")
+    return me // (2 * NX), (me // 2) % NX, me % 2, lax.axis_index("head")
+
+
+def device_at(z, x, core, y):
+    return ((z * NX + x) * 2 + core, y)
+
+
+def greet(nz, ny):
+    z, x, core, y = place_of()
+    barrier = pltpu.get_barrier_semaphore()
+
+    def hello(device):
+        pl.semaphore_signal(barrier, inc=1, device_id=device, device_id_type=MESH)
+
+    for dy in range(ny):
+        for dc in range(2):
+            if dy or dc:
+                hello(device_at(z, x, (core + dc) % 2, (y + dy) % ny))
+    hello(device_at(z, 1 - x, core, y))
+
+    @pl.when(z > 0)
+    def _():
+        hello(device_at(z - 1, x, core, y))
+
+    @pl.when(z < nz - 1)
+    def _():
+        hello(device_at(z + 1, x, core, y))
+
+    @pl.when((z == 0) | (z == nz - 1))
+    def _():
+        pl.semaphore_wait(barrier, 2 * ny + 1)
+
+    @pl.when((z > 0) & (z < nz - 1))
+    def _():
+        pl.semaphore_wait(barrier, 2 * ny + 2)
+
+
+def remote(src, dst, sems, index, device):
+    return pltpu.make_async_remote_copy(
+        src_ref=src, dst_ref=dst, send_sem=sems.at[(0, *index)], recv_sem=sems.at[(1, *index)],
+        device_id=device, device_id_type=MESH,
+    )
+
+
+def aligned(index, size):
+    return pl.ds(pl.multiple_of(index * size, size), size)
+
+
+def spread_kernel(
+    nz, ny, q_in, o_in, k_in, v_in, d_in, q_out, o_out, k_out, v_out, d_out,
+    local_sems, pair_sems, group_sems, up_sems, down_sems, side_sems,
+):
+    z, x, core, y = place_of()
+    other = 1 - core
+    own = k_in.shape[0]
+    rows = 2 * own
+    share = d_in.shape[0]
+    sibling = device_at(z, x, other, y)
+    greet(nz, ny)
+
+    chip_row = (z * NX + x) * rows
+    mine = pl.ds(pl.multiple_of(chip_row + core * own, own), own)
+    pairs, locals_ = [], []
+    for n, (src, dst, where) in enumerate((
+        (k_in, k_out, mine), (v_in, v_out, mine),
+        (q_in, q_out, aligned(core, own)), (o_in, o_out, aligned(core, own)),
+    )):
+        width = dst.shape[1]
+        pairs.append(remote(
+            src.at[:, aligned(other, width)], dst.at[where, :], pair_sems, (n,), sibling
+        ))
+        locals_.append(pltpu.make_async_copy(
+            src.at[:, aligned(core, width)], dst.at[where, :], local_sems.at[n]
+        ))
+    width = d_out.shape[1]
+    group = []
+    d_rows = aligned(core * ny + y, share)
+    for dy in range(ny):
+        for dc in range(2):
+            yy, cc = (y + dy) % ny, (core + dc) % 2
+            src = d_in.at[:, aligned(yy * 2 + cc, width)]
+            if dy or dc:
+                group.append(remote(
+                    src, d_out.at[d_rows, :], group_sems, (dy, dc), device_at(z, x, cc, yy)
+                ))
+            else:
+                locals_.append(pltpu.make_async_copy(src, d_out.at[d_rows, :], local_sems.at[4]))
+
+    for n in range(2):
+        pairs[n].start()
+        locals_[n].start()
+    for copy in reversed(group):
+        copy.start()
+    for n in range(2):
+        locals_[n].wait()
+        pairs[n].wait_recv()
+
+    def hop(n, zz, sems, device):
+        ref = (k_out, v_out)[n].at[aligned(zz * NX + x, rows), :]
+        return remote(ref, ref, sems, (n, zz), device)
+
+    def up(n, zz):
+        return hop(n, zz, up_sems, device_at(z + 1, x, core, y))
+
+    def down(n, zz):
+        return hop(n, zz, down_sems, device_at(z - 1, x, core, y))
+
+    def side(n, zz):
+        return hop(n, zz, side_sems, device_at(z, 1 - x, core, y))
+
+    def side_in(n, zz):
+        ref = (k_out, v_out)[n].at[aligned(zz * NX + 1 - x, rows), :]
+        return remote(ref, ref, side_sems, (n, zz), device_at(z, 1 - x, core, y))
+
+    for n in range(2):
+        @pl.when(z < nz - 1)
+        def _():
+            up(n, z).start()
+
+        @pl.when(z > 0)
+        def _():
+            down(n, z).start()
+
+        side(n, z).start()
+    for n in range(2, 4):
+        pairs[n].start()
+        locals_[n].start()
+    locals_[4].start()
+
+    for step in range(1, nz):
+        for n in range(2):
+            @pl.when(z - step >= 0)
+            def _():
+                up(n, z - step).wait_recv()
+
+                @pl.when(z < nz - 1)
+                def _():
+                    up(n, z - step).start()
+
+                side(n, z - step).start()
+
+            @pl.when(z + step < nz)
+            def _():
+                down(n, z + step).wait_recv()
+
+                @pl.when(z > 0)
+                def _():
+                    down(n, z + step).start()
+
+                side(n, z + step).start()
+
+    for n in range(2):
+        for zz in range(nz):
+            side_in(n, zz).wait_recv()
+            side(n, zz).wait_send()
+
+            @pl.when((zz <= z) & (z < nz - 1))
+            def _():
+                up(n, zz).wait_send()
+
+            @pl.when((zz >= z) & (z > 0))
+            def _():
+                down(n, zz).wait_send()
+
+        pairs[n].wait_send()
+        pairs[n + 2].wait()
+        locals_[n + 2].wait()
+    locals_[4].wait()
+    for copy in group:
+        copy.wait()
+
+
+def spread(q, o, k, v, d, ctx, ny):
+    nz = ctx // (2 * NX)
+    rows = 2 * q.shape[0]
+    seq = k.shape[0] * ctx
+
+    def like(height, x, parts):
+        return jax.ShapeDtypeStruct((height, x.shape[1] // parts), x.dtype)
+
+    anywhere = pl.BlockSpec(memory_space=pl.ANY)
+    dma = pltpu.SemaphoreType.DMA
+    return pl.pallas_call(
+        functools.partial(spread_kernel, nz, ny),
+        out_shape=[like(rows, q, 2), like(rows, o, 2), like(seq, k, 2), like(seq, v, 2),
+                   like(rows, d, 2 * ny)],
+        in_specs=[anywhere] * 5,
+        out_specs=[anywhere] * 5,
+        scratch_shapes=[
+            dma((5,)), dma((2, 4)), dma((2, ny, 2)), dma((2, 2, nz)), dma((2, 2, nz)), dma((2, 2, nz)),
+        ],
+        compiler_params=pltpu.CompilerParams(collective_id=0, has_side_effects=True),
+        name="spread",
+    )(q, o, k, v, d)
+
+
+def fold_kernel(
+    nz, ny, dk_in, dv_in, dq_in, gk_out, gv_out, gq_out,
+    side_buf, up_buf, down_buf, out_buf, fin,
+    local_sems, pair_sems, group_sems, up_sems, down_sems, side_sems,
+):
+    z, x, core, y = place_of()
+    other = 1 - core
+    rows = fin.shape[1]
+    own = rows // 2
+    share = gq_out.shape[0]
+    parts = (dk_in, dv_in)
+    greet(nz, ny)
+
+    def side(n, zz):
+        return remote(
+            parts[n].at[aligned(zz * NX + 1 - x, rows), :], side_buf.at[n, zz], side_sems, (n, zz),
+            device_at(z, 1 - x, core, y),
+        )
+
+    def up(n, zz):
+        return remote(
+            out_buf.at[n, zz], up_buf.at[n, zz], up_sems, (n, zz), device_at(z + 1, x, core, y)
+        )
+
+    def down(n, zz):
+        return remote(
+            out_buf.at[n, zz], down_buf.at[n, zz], down_sems, (n, zz), device_at(z - 1, x, core, y)
+        )
+
+    order = []
+    for far in range(nz // 2):
+        order.append(jnp.where(z < nz // 2, nz - 1 - far, far))
+        order.append(jnp.where(z < nz // 2, far, nz - 1 - far))
+
+    width = dq_in.shape[1]
+    group = []
+    for dy in range(ny):
+        for dc in range(2):
+            yy, cc = (y + dy) % ny, (core + dc) % 2
+            src = dq_in.at[aligned(cc * ny + yy, share), :]
+            dst = gq_out.at[:, aligned(y * 2 + core, width)]
+            if dy or dc:
+                group.append(remote(src, dst, group_sems, (dy, dc), device_at(z, x, cc, yy)))
+            else:
+                keep = pltpu.make_async_copy(src, dst, local_sems.at[2])
+    for zz in order:
+        for n in range(2):
+            side(n, zz).start()
+    for copy in reversed(group):
+        copy.start()
+    keep.start()
+
+    def total(n, zz):
+        mine = parts[n][aligned(zz * NX + x, rows), :].astype(jnp.float32)
+        return mine + side_buf[n, zz].astype(jnp.float32)
+
+    for zz in order:
+        for n in range(2):
+            @pl.when(zz > z)
+            def _():
+                side(n, zz).wait_recv()
+
+                @pl.when(z == 0)
+                def _():
+                    out_buf[n, zz] = total(n, zz).astype(jnp.bfloat16)
+
+                @pl.when(z > 0)
+                def _():
+                    up(n, zz).wait_recv()
+                    out_buf[n, zz] = (
+                        total(n, zz) + up_buf[n, zz].astype(jnp.float32)
+                    ).astype(jnp.bfloat16)
+
+                up(n, zz).start()
+
+            @pl.when(zz < z)
+            def _():
+                side(n, zz).wait_recv()
+
+                @pl.when(z == nz - 1)
+                def _():
+                    out_buf[n, zz] = total(n, zz).astype(jnp.bfloat16)
+
+                @pl.when(z < nz - 1)
+                def _():
+                    down(n, zz).wait_recv()
+                    out_buf[n, zz] = (
+                        total(n, zz) + down_buf[n, zz].astype(jnp.float32)
+                    ).astype(jnp.bfloat16)
+
+                down(n, zz).start()
+
+    ends = []
+    for n, out in enumerate((gk_out, gv_out)):
+        side(n, z).wait_recv()
+
+        @pl.when(z == 0)
+        def _():
+            down(n, z).wait_recv()
+            fin[n] = (total(n, z) + down_buf[n, z].astype(jnp.float32)).astype(jnp.bfloat16)
+
+        @pl.when(z == nz - 1)
+        def _():
+            up(n, z).wait_recv()
+            fin[n] = (total(n, z) + up_buf[n, z].astype(jnp.float32)).astype(jnp.bfloat16)
+
+        @pl.when((z > 0) & (z < nz - 1))
+        def _():
+            up(n, z).wait_recv()
+            down(n, z).wait_recv()
+            fin[n] = (
+                total(n, z) + up_buf[n, z].astype(jnp.float32) + down_buf[n, z].astype(jnp.float32)
+            ).astype(jnp.bfloat16)
+
+        columns = aligned(core, fin.shape[2])
+        pair = remote(
+            fin.at[n, aligned(other, own), :], out.at[:, columns], pair_sems, (n,),
+            device_at(z, x, other, y),
+        )
+        here = pltpu.make_async_copy(
+            fin.at[n, aligned(core, own), :], out.at[:, columns], local_sems.at[n]
+        )
+        pair.start()
+        here.start()
+        ends += [pair, here]
+
+    for copy in ends + group + [keep]:
+        copy.wait()
+    for n in range(2):
+        for zz in range(nz):
+            side(n, zz).wait_send()
+
+            @pl.when(zz > z)
+            def _():
+                up(n, zz).wait_send()
+
+            @pl.when(zz < z)
+            def _():
+                down(n, zz).wait_send()
+
+
+def fold(dk, dv, dq, ctx, ny):
+    nz = ctx // (2 * NX)
+    rows = dq.shape[0]
+    own = rows // 2
+    width = dk.shape[1]
+    anywhere = pl.BlockSpec(memory_space=pl.ANY)
+    whole = pl.BlockSpec(memory_space=pltpu.VMEM)
+    dma = pltpu.SemaphoreType.DMA
+    buffers = pltpu.VMEM((2, nz, rows, width), jnp.bfloat16)
+    kv_out = jax.ShapeDtypeStruct((own, 2 * width), jnp.bfloat16)
+    return pl.pallas_call(
+        functools.partial(fold_kernel, nz, ny),
+        out_shape=[kv_out, kv_out,
+                   jax.ShapeDtypeStruct((rows // (2 * ny), dq.shape[1] * 2 * ny), jnp.bfloat16)],
+        in_specs=[whole, whole, anywhere],
+        out_specs=[anywhere] * 3,
+        scratch_shapes=[
+            buffers, buffers, buffers, buffers, pltpu.VMEM((2, rows, width), jnp.bfloat16),
+            dma((3,)), dma((2, 2)), dma((2, ny, 2)), dma((2, 2, nz)), dma((2, 2, nz)), dma((2, 2, nz)),
+        ],
+        compiler_params=pltpu.CompilerParams(
+            collective_id=1, has_side_effects=True, vmem_limit_bytes=32 * 2**20
+        ),
+        name="fold",
+    )(dk, dv, dq)
+
+
 def row_terms_of(terms, kv_heads, span):
     rows = terms.shape[1]
     cut = terms.reshape(kv_heads, GROUPS, rows // span, span)
@@ -167,13 +537,19 @@
             x, "ctx", split_axis=split, concat_axis=concat, axis_index_groups=chip_groups, tiled=True
         )
 
-    q = to_heads(query_rows)
-    o = to_heads(attn_output)
+    ny = lax.axis_size("head")
+    by_kernels = cores == 2 and ctx % (4 * NX) == 0
     lse = to_heads(log_norms, 0, 1)
-    d = to_heads(lax.all_to_all(grad_output, "head", split_axis=1, concat_axis=0, tiled=True))
-    kv = jnp.concatenate([to_heads(key_rows), to_heads(value_rows)], axis=1)
-    kv = lax.all_gather(kv, "ctx", axis=0, axis_index_groups=ring_groups, tiled=True)
-    half = kv.shape[1] // 2
+    if by_kernels:
+        q, o, k, v, d = spread(query_rows, attn_output, key_rows, value_rows, grad_output, ctx, ny)
+    else:
+        q = to_heads(query_rows)
+        o = to_heads(attn_output)
+        d = to_heads(lax.all_to_all(grad_output, "head", split_axis=1, concat_axis=0, tiled=True))
+        kv = jnp.concatenate([to_heads(key_rows), to_heads(value_rows)], axis=1)
+        kv = lax.all_gather(kv, "ctx", axis=0, axis_index_groups=ring_groups, tiled=True)
+        k, v = kv[:, :kv.shape[1] // 2], kv[:, kv.shape[1] // 2:]
+    half = k.shape[1]
     kv_heads = half // HD
     rows = q.shape[0]
     delta = jnp.sum(
@@ -184,10 +560,12 @@
     slot_of = jnp.argsort(span_order).astype(jnp.int32)
     my_spans = lax.dynamic_slice_in_dim(span_order, (me // cores) * slots, slots)
     dq, dk, dv = attend(
-        slot_of, my_spans, q, d, kv[:, :half], kv[:, half:],
+        slot_of, my_spans, q, d, k, v,
         row_terms_of(lse * LOG2E, kv_heads, span), row_terms_of(delta, kv_heads, span),
-        span, jnp.float32,
+        span, jnp.bfloat16 if by_kernels else jnp.float32,
     )
+    if by_kernels:
+        return tuple(fold(dk, dv, dq, ctx, ny)[n] for n in (2, 0, 1))
     dkv = jnp.concatenate([dk, dv], axis=1)
     dkv = lax.psum_scatter(dkv, "ctx", scatter_dimension=0, axis_index_groups=ring_groups, tiled=True)
     dkv = dkv.astype(jnp.bfloat16)

time: 280 us -> 266 us (0.950)
  Pallas kernels: 49.9 us -> 248 us
  waiting for transfers between devices: 103 us -> 0.01 us
  blocking collectives: 44.9 us -> 0 us
  local copies, waits for them, and re-layouts: 26.4 us -> 3.84 us
  starting transfers between devices: 21.3 us -> 3.93 us
  between operations: 14.2 us -> 0.77 us
  other arithmetic: 14.7 us -> 4.97 us
    pallas_call x0 -> x4, Pallas kernels: none -> 202 us  [the longest x3 133 us: fold(): pl.pallas_call(functools.partial(fold_kernel, nz, ny), out_shape=[kv_out,...]
    reduce_scatter x1 -> x0, waiting for transfers between devices: 83.1 us -> none  [per_device(): lax.psum_scatter(dkv, 'ctx', scatter_dimension=0, axis_index_groups=ring_...]
    all_to_all x6 -> x0, blocking collectives: 44.9 us -> none  [the longest x5 23.3 us: to_heads(): lax.all_to_all(x, 'ctx', split_axis=split, concat_axis=concat, axis_index...]
    all_to_all x12 -> x0, local copies, waits for them, and re-layouts: 16.3 us -> none  [the longest x9 12.6 us: to_heads(): lax.all_to_all(x, 'ctx', split_axis=split, concat_axis=concat, axis_index...]
    all_to_all x1 -> x0, waiting for transfers between devices: 14 us -> none  [per_device(): lax.all_to_all(grad_output, 'head', split_axis=1, concat_axis=0, tiled=True)]
    all_to_all x4 -> x1, starting transfers between devices: 17.4 us -> 3.93 us  [to_heads(): lax.all_to_all(x, 'ctx', split_axis=split, concat_axis=concat, axis_index...]
    concatenate x2 -> x0, other arithmetic: 7.19 us -> none  [the longest x1 6.37 us: per_device(): dkv = jnp.concatenate([dk, dv], axis=1)]
    all_gather x1 -> x0, waiting for transfers between devices: 5.9 us -> none  [per_device(): lax.all_gather(kv, 'ctx', axis=0, axis_index_groups=ring_groups, tiled=True)]
  transfers between devices with their start and end apart: 7 -> 1, of which waited for: 4 -> 0; matrix products, arithmetic and copies ran while one was open for 8% -> 2% of each run, Pallas kernels for 0% -> 27%
where the time goes in v2:
time: 266 us; the launch traced here: 261 us
  Pallas kernels  248 us (93%)
  other arithmetic  4.97 us (2%)
  starting transfers between devices  3.93 us (1%)
  local copies, waits for them, and re-layouts  3.84 us (1%)
    pallas_call x3, Pallas kernels, fold(): pl.pallas_call(functools.partial(fold_kernel, nz, ny), out_shape=[kv_out,...  133 us
    pallas_call x1, Pallas kernels, spread(): pl.pallas_call(functools.partial(spread_kernel, nz, ny), out_shape=[like(...  69.6 us
    pallas_call x1, Pallas kernels, attend(): pl.pallas_call(attend_kernel, grid_spec=pltpu.PrefetchScalarGridSpec(num_...  45.3 us
  transfers between devices with their start and end apart: 1, of which 0 were waited for; matrix products, arithmetic and copies ran while one was open for 2% of the time, Pallas kernels for 27%

profile of v2, /device:TPU:9, one launch (start us, length us, event | category | flops | bytes accessed | tf_op | source)
XLA Modules:
  0.0 261.2 jit_solution(3254240566353446490)
XLA Ops:
  0.6 3.9 %all-to-all-start = ((f32[2,16,192]{2,1,0:T(8,128)}), f32[2,16,192]{2,1,0:T(8,128)S(1)}, u32[]{:S(2)}, u32[]{:S(2)}) async-start(f32[2,16,192]{2,1,0:T(8,128)} %bitcast.17), calls=%async_computation | async-start | bytes 65536 | tf_op jit(solution)/shard_map/all_to_all | solution.py:536
  4.6 69.6 %spread.1 = (bf16[384,2048]{1,0:T(8,128)(2,1)}, bf16[384,2048]{1,0:T(8,128)(2,1)}, bf16[3072,256]{1,0:T(8,128)(2,1)}, bf16[3072,256]{1,0:T(8,128)(2,1)}, bf16[384,2048]{1,0:T(8,128)(2,1)}) custom-call(bf16[192,4096]{1,0:T(8,128)(2,1)} %q_in.1, bf16[192,4096]{1,0:T(8,128)(2,1)} %o_in.1, bf16[192,512]{1,0:T(8,128)(2,1)} %k_in.1, bf16[192,512]{1,0:T(8,128)(2,1)} %v_in.1, ...), custom_call_target="tpu_custom_call" | custom-call | tf_op jit(solution)/shard_map/spread/pallas_call | solution.py:336
  74.2 2.5 multiply_bitcast_fusion
  76.7 0.7 copy.17
  77.4 0.0 copy-start
  77.4 0.9 reduce_sum.9
  78.3 0.1 copy.15
  78.3 0.1 reshape.27
  78.5 0.1 reshape.28.delta_ref
  78.6 0.0 all-to-all-done
  78.6 0.1 mul.23
  78.7 0.1 reshape.25.lse_ref
  78.9 0.1 broadcast_in_dim_tile.3.base_ref
  78.9 0.0 copy-done
  78.9 0.1 dynamic_slice.3.my_span_ref
  79.0 1.6 sort.17
  80.6 45.3 %attend.1 = (bf16[384,2048]{1,0:T(8,128)(2,1)S(1)}, bf16[3072,256]{1,0:T(8,128)(2,1)S(1)}, bf16[3072,256]{1,0:T(8,128)(2,1)S(1)}) custom-call(s32[32]{0:T(128)S(1)} %get-tuple-element.15.slot_of_ref, s32[4]{0:T(128)S(1)} %dynamic_slice.3.my_span_ref, bf16[384,2048]{1,0:T(8,128)(2,1)} %get-tuple-element.16.q_ref, bf16[384,2048]{1,0:T(8,128)(2,1)} %get-tuple-element.17.d_ref, ...), custom_call_target="tpu_custom_call" | custom-call | flops 16911433728 | bytes 16777216 | tf_op jit(solution)/shard_map/attend/pallas_call | solution.py:110
  126.0 44.1 %fold.5 = (bf16[192,512]{1,0:T(8,128)(2,1)}, bf16[192,512]{1,0:T(8,128)(2,1)S(1)}, bf16[96,8192]{1,0:T(8,128)(2,1)}) custom-call(bf16[3072,256]{1,0:T(8,128)(2,1)S(1)} %get-tuple-element.21.dk_in, bf16[3072,256]{1,0:T(8,128)(2,1)S(1)} %get-tuple-element.22.dv_in, bf16[384,2048]{1,0:T(8,128)(2,1)S(1)} %get-tuple-element.23.dq_in), custom_call_target="tpu_custom_call" | custom-call | tf_op jit(solution)/shard_map/fold/pallas_call | solution.py:501
  170.0 44.3 %fold.4 = (bf16[192,512]{1,0:T(8,128)(2,1)S(1)}, bf16[192,512]{1,0:T(8,128)(2,1)}, bf16[96,8192]{1,0:T(8,128)(2,1)}) custom-call(bf16[3072,256]{1,0:T(8,128)(2,1)S(1)} %get-tuple-element.21.dk_in, bf16[3072,256]{1,0:T(8,128)(2,1)S(1)} %get-tuple-element.22.dv_in, bf16[384,2048]{1,0:T(8,128)(2,1)S(1)} %get-tuple-element.23.dq_in), custom_call_target="tpu_custom_call" | custom-call | tf_op jit(solution)/shard_map/fold/pallas_call | solution.py:501
  214.4 44.3 %fold.3 = (bf16[192,512]{1,0:T(8,128)(2,1)}, bf16[192,512]{1,0:T(8,128)(2,1)}, bf16[96,8192]{1,0:T(8,128)(2,1)S(1)}) custom-call(bf16[3072,256]{1,0:T(8,128)(2,1)S(1)} %get-tuple-element.21.dk_in, bf16[3072,256]{1,0:T(8,128)(2,1)S(1)} %get-tuple-element.22.dv_in, bf16[384,2048]{1,0:T(8,128)(2,1)S(1)} %get-tuple-element.23.dq_in), custom_call_target="tpu_custom_call" | custom-call | tf_op jit(solution)/shard_map/fold/pallas_call | solution.py:501
  258.7 1.1 copy.21
  259.8 0.7 copy.22
  260.5 0.7 copy.23
  (6 shorter events, 0.0 us)
Async XLA Ops:
  0.6 77.9 %all-to-all-start = ((f32[2,16,192]{2,1,0:T(8,128)}), f32[2,16,192]{2,1,0:T(8,128)S(1)}, u32[]{:S(2)}, u32[]{:S(2)}) async-start(f32[2,16,192]{2,1,0:T(8,128)} %bitcast.17), calls=%async_computation | async-start | bytes 65536 | tf_op jit(solution)/shard_map/all_to_all | solution.py:536
  77.4 1.6 copy-start
